TPU v7x, 512 devices: a whole 4x8x8 slice. The times are simulated.
512 devices in a mesh: row: 128 (over x, y_lo, z), rep: 4 (over y_hi, core).
Axes of the slice: x: 4, y: 8 (y_hi: 2, y_lo: 4; y = y_hi * 4 + y_lo), z: 8, core: 2. Of those that a mesh axis runs over, the one named last changes fastest.
Arguments:
- pair: bfloat16 [2048, 512, 128], P(('rep', 'row')), parts along dimension 0, may hold values from -6 to 6
- token_mask: int32 [2048], P('rep'), parts along dimension 0, may hold values from 0 to 1, as said below
- start_gain: float32 [128], replicated, may hold values from 0.5 to 1.5
- start_proj: bfloat16 [128, 512], replicated, may hold values from -1 to 1
- start_bias: bfloat16 [128, 4], replicated, may hold values from -0.5 to 0.5
- start_out: bfloat16 [128, 128], replicated, may hold values from -0.5 to 0.5
- end_gain: float32 [128], replicated, may hold values from 0.5 to 1.5
- end_proj: bfloat16 [128, 512], replicated, may hold values from -1 to 1
- end_bias: bfloat16 [128, 4], replicated, may hold values from -0.5 to 0.5
- end_out: bfloat16 [128, 128], replicated, may hold values from -0.5 to 0.5
Outputs:
- updated: bfloat16 [2048, 512, 128], P(('rep', 'row')), parts along dimension 0
There are 4 independent parts, one for each index of `rep`. A program takes and returns all parts, laid end to end along the dimension named above; an argument that names none is the same for every part. Nothing has to cross between parts.
Inputs may be any that keep to these rules, and one draw needn't show every extreme that they name: `token_mask`: exactly 448 entries are 1, at positions drawn from the seed.
All inputs are finite; a program needn't handle non-finite values.
Results may differ from a plain program's by a relative error of at most 0.006.
Values may be sent and summed in bfloat16 or wider, within the bound.
A program may use at most 64 MiB of HBM per device.

v0:
```python
import math

import jax
import jax.numpy as jnp
from jax import lax
from jax.sharding import PartitionSpec as P


def layer_norm(values, gain):
    wide = values.astype(jnp.float32)
    center = wide - jnp.mean(wide, axis=-1, keepdims=True)
    spread = jnp.mean(center * center, axis=-1, keepdims=True)
    return (center * lax.rsqrt(spread + 1e-05) * gain).astype(jnp.bfloat16)


def project(normed, w_proj):
    return jnp.dot(normed, w_proj, preferred_element_type=jnp.float32).astype(jnp.bfloat16)


def pair_bias(normed, w_bias):
    return jnp.einsum("rnc,ch->hrn", normed, w_bias, preferred_element_type=jnp.float32).astype(
        jnp.bfloat16
    )


def attend_block(proj, bias_block, start, mask_term, heads):
    rows = proj.shape[0]
    count = proj.shape[1]
    width = proj.shape[2] // 4
    head_size = width // heads
    queries = bias_block.shape[1]
    query = lax.dynamic_slice_in_dim(proj[:, :, :width], start, queries, 1).reshape(
        rows, queries, heads, head_size
    )
    keys = proj[:, :, width : 2 * width].reshape(rows, count, heads, head_size)
    values = proj[:, :, 2 * width : 3 * width].reshape(rows, count, heads, head_size)
    gates = lax.dynamic_slice_in_dim(proj[:, :, 3 * width :], start, queries, 1)
    scores = jnp.einsum("rjhd,rkhd->rhjk", query, keys, preferred_element_type=jnp.float32) * (
        1.0 / math.sqrt(head_size)
    )
    scores = scores + bias_block.astype(jnp.float32)[None] + mask_term
    scores = scores - jnp.max(scores, axis=-1, keepdims=True)
    expo = jnp.exp(scores)
    probs = (expo / jnp.sum(expo, axis=-1, keepdims=True)).astype(jnp.bfloat16)
    attended = jnp.einsum(
        "rhjk,rkhd->rjhd", probs, values, preferred_element_type=jnp.float32
    ).reshape(rows, queries, width)
    return (jax.nn.sigmoid(gates.astype(jnp.float32)) * attended).astype(jnp.bfloat16)


def attend_all(proj, slab_fn, mask_term, heads):
    rows = proj.shape[0]
    total = proj.shape[1]
    block = math.gcd(total, max(64, 512 // rows))

    def one_block(start):
        return attend_block(proj, slab_fn(start, block), start, mask_term, heads)

    pieces = lax.map(one_block, jnp.arange(total // block, dtype=jnp.int32) * block)
    return jnp.transpose(pieces, (1, 0, 2, 3)).reshape(rows, total, pieces.shape[3])


def body(
    pair,
    token_mask,
    start_gain,
    start_proj,
    start_bias,
    start_out,
    end_gain,
    end_proj,
    end_bias,
    end_out,
):
    mask_term = (token_mask.astype(jnp.float32) - 1.0) * 1000000000.0
    heads = start_bias.shape[1]
    normed = layer_norm(pair, start_gain)
    bias_rows = pair_bias(normed, start_bias)
    whole_start = lax.all_gather(bias_rows, "row", axis=1, tiled=True)
    proj = project(normed, start_proj)

    def start_slab(start, block):
        return lax.dynamic_slice_in_dim(whole_start, start, block, 1)

    hidden = attend_all(proj, start_slab, mask_term, heads)
    first = (
        pair.astype(jnp.float32) + jnp.dot(hidden, start_out, preferred_element_type=jnp.float32)
    ).astype(jnp.bfloat16)
    flipped = lax.all_to_all(
        jnp.swapaxes(first, 0, 1), "row", split_axis=0, concat_axis=1, tiled=True
    )
    normed_flip = layer_norm(flipped, end_gain)
    bias_flip = pair_bias(normed_flip, end_bias)
    whole_end = lax.all_gather(bias_flip, "row", axis=1, tiled=True)

    def end_slab(start, block):
        return lax.dynamic_slice_in_dim(whole_end, start, block, 1)

    proj_flip = project(normed_flip, end_proj)
    hidden_flip = attend_all(proj_flip, end_slab, mask_term, heads)
    late = jnp.dot(hidden_flip, end_out, preferred_element_type=jnp.float32).astype(jnp.bfloat16)
    returned = lax.all_to_all(
        jnp.swapaxes(late, 0, 1), "row", split_axis=0, concat_axis=1, tiled=True
    )
    return (first.astype(jnp.float32) + returned.astype(jnp.float32)).astype(jnp.bfloat16)


def solution(mesh):
    return jax.shard_map(
        body,
        mesh=mesh,
        in_specs=(P(("rep", "row"), None, None), P("rep"), P(), P(), P(), P(), P(), P(), P(), P()),
        out_specs=P(("rep", "row"), None, None),
        check_vma=False,
    )
```

profile of v0, /device:TPU:56, one launch (start us, length us, event | category | flops | bytes accessed | tf_op | source)
XLA Modules:
  0.0 1569.3 jit_solution(1974119983171814008)
XLA Ops:
  12.0 3.2 convolution_convert_fusion.1
  15.2 2.8 copy.55
  18.0 633.1 %all-gather.3.cloned.1.call-done = bf16[4,512,512]{2,0,1:T(4,128)(2,1)} async-done(((bf16[4,4,512]{2,0,1:T(4,128)(2,1)}), bf16[4,512,512]{2,0,1:T(4,128)(2,1)}) %all-gather.3.cloned.1.call-update) | async-done | bytes 2097168 | tf_op jit(solution)/shard_map/all_gather | solution.py:79
  652.1 58.8 %while.20 = (s32[]{:T(128)}, bf16[4,4,128,128]{3,2,0,1:T(8,128)(2,1)}, bf16[4,512,512]{1,2,0:T(8,128)(2,1)S(1)}, s32[4]{0:T(128)S(1)}, bf16[4,512,512]{2,0,1:T(4...) while((s32[]{:T(128)}, bf16[4,4,128,128]{3,2,0,1:T(8,128)(2,1)}, ...), condition=%wide.region_5.6_spmd, body=%wide.region_2.5_spmd.sunk | while | flops 142213632 | bytes 19024536 | solution.py:59
  657.1 4.5 fusion.73
  661.6 3.2 fusion.74
  671.8 4.6 fusion.73
  676.3 3.2 fusion.74
  686.5 4.5 fusion.73
  691.0 3.2 fusion.74
  701.2 4.5 fusion.73
  705.7 3.2 fusion.74
  713.1 75.6 %all_to_all.8 = bf16[512,4,128]{2,1,0:T(4,128)(2,1)S(1)} all-to-all(bf16[512,4,128]{2,1,0:T(4,128)(2,1)S(1)} %copy.58), channel_id=1, replica_groups=mesh['row'=128,'rep'=4] {'row'}, dimensions={0} | all-to-all | bytes 1048576 | tf_op jit(solution)/shard_map/all_to_all | solution.py:89
  798.1 624.3 %all-gather.5.cloned.1.call-done = bf16[4,512,512]{2,0,1:T(4,128)(2,1)} async-done(((bf16[4,4,512]{2,0,1:T(4,128)(2,1)}), bf16[4,512,512]{2,0,1:T(4,128)(2,1)}) %all-gather.5.cloned.1.call-update) | async-done | bytes 2097168 | tf_op jit(solution)/shard_map/all_gather | solution.py:94
  1423.3 60.4 %while.21 = (s32[]{:T(128)}, bf16[4,4,128,128]{3,2,0,1:T(8,128)(2,1)}, bf16[4,512,512]{1,2,0:T(8,128)(2,1)S(1)}, s32[4]{0:T(128)S(1)}, bf16[4,512,512]{2,0,1:T(4...) while((s32[]{:T(128)}, bf16[4,4,128,128]{3,2,0,1:T(8,128)(2,1)}, ...), condition=%wide.region_11.12_spmd, body=%wide.region_8.11_spmd.sunk | while | flops 142213632 | bytes 19024536 | solution.py:59
  1428.7 4.6 fusion.80
  1433.3 3.2 fusion.81
  1443.8 4.6 fusion.80
  1448.4 3.2 fusion.81
  1459.0 4.6 fusion.80
  1463.5 3.2 fusion.81
  1474.1 4.6 fusion.80
  1478.6 3.2 fusion.81
  1485.5 75.9 %all_to_all.9 = bf16[512,4,128]{2,1,0:T(4,128)(2,1)S(1)} all-to-all(bf16[512,4,128]{2,1,0:T(4,128)(2,1)S(1)} %copy.70), channel_id=1, replica_groups=mesh['row'=128,'rep'=4] {'row'}, dimensions={0} | all-to-all | bytes 1048576 | tf_op jit(solution)/shard_map/all_to_all | solution.py:102
  (114 shorter events, 63.5 us)
Async XLA Ops:
  6.5 5.5 copy-start
  6.5 644.6 %all-gather.3.cloned.1.call-start = ((), (), s32[]{:S(2)}) async-start(), calls=%async_computation.2 | async-start | bytes 2113536 | tf_op jit(solution)/shard_map/all_gather | solution.py:79
  9.5 8.5 copy-start.6
  12.0 1410.5 %all-gather.5.cloned.1.call-start = ((), (), s32[]{:S(2)}) async-start(), calls=%async_computation.3 | async-start | bytes 2113536 | tf_op jit(solution)/shard_map/all_gather | solution.py:94
  652.1 58.8 %copy-start.4 = (bf16[128,128]{1,0:T(8,128)(2,1)S(1)}, bf16[128,128]{1,0:T(8,128)(2,1)}, u32[]{:S(2)}) copy-start(bf16[128,128]{1,0:T(8,128)(2,1)} %param.19) | copy-start | bytes 98308
  712.3 0.8 copy-start.1
  788.8 3.2 copy-start.7
  788.8 3.2 copy-start.8
  788.9 4.4 copy-start.3
  1423.3 60.4 %copy-start.5 = (bf16[128,128]{1,0:T(8,128)(2,1)S(1)}, bf16[128,128]{1,0:T(8,128)(2,1)}, u32[]{:S(2)}) copy-start(bf16[128,128]{1,0:T(8,128)(2,1)} %param.23) | copy-start | bytes 98308
  1483.7 77.8 %copy-start.2 = (bf16[4,512,128]{2,1,0:T(8,128)(2,1)S(1)}, bf16[4,512,128]{2,1,0:T(8,128)(2,1)}, u32[]{:S(2)}) copy-start(bf16[4,512,128]{2,1,0:T(8,128)(2,1)} %copy-done.1) | copy-start | bytes 1572868
Sparse Core Ops, SparseCore 0:
  12.1 639.0 all-gather.2
  793.4 628.9 all-gather.4
where the time goes:
time: 1570 us
  waiting for transfers between devices  1260 us (80%)
  blocking collectives  152 us (10%)
  matrix products  73.5 us (5%)
  local copies, waits for them, and re-layouts  41.3 us (3%)
  other arithmetic  16.4 us (1%)
    all_gather x1, waiting for transfers between devices, body(): whole_start = lax.all_gather(bias_rows, 'row', axis=1, tiled=True)  633 us
    all_gather x1, waiting for transfers between devices, body(): whole_end = lax.all_gather(bias_flip, 'row', axis=1, tiled=True)  624 us
    all_to_all x1, blocking collectives, body(): lax.all_to_all(jnp.swapaxes(late, 0, 1), 'row', split_axis=0, concat_axis...  75.9 us
    all_to_all x1, blocking collectives, body(): lax.all_to_all(jnp.swapaxes(first, 0, 1), 'row', split_axis=0, concat_axi...  75.6 us
    sub x8, matrix products, attend_block(): scores = scores - jnp.max(scores, axis=-1, keepdims=True)  36.4 us
  transfers between devices with their start and end apart: 2, of which 2 were waited for; matrix products, arithmetic and copies ran while one was open for 1% of the time, Pallas kernels for 0%

commit v1 on v0

v1 whole, which is shorter than its diff:
```python
import functools
import math

import jax
import jax.numpy as jnp
from jax import lax
from jax.experimental import pallas as pl
from jax.experimental.pallas import tpu as pltpu
from jax.sharding import PartitionSpec as P

MESH = pl.DeviceIdType.MESH
LOG2E = 1.4426950408889634
F32 = jnp.float32
BF16 = jnp.bfloat16
ROWS = 4
HEADS = 4
CH = ROWS * HEADS


def iota(shape, dim):
    return lax.broadcasted_iota(jnp.int32, shape, dim)


def nt(a, b):
    return lax.dot_general(a, b, (((1,), (1,)), ((), ())), preferred_element_type=F32)


def mm(a, b):
    return jnp.dot(a, b, preferred_element_type=F32)


def ln(wide, gain):
    center = wide - jnp.mean(wide, axis=-1, keepdims=True)
    spread = jnp.mean(center * center, axis=-1, keepdims=True)
    return (center * lax.rsqrt(spread + 1e-05) * gain).astype(BF16)


def kernel(
    dims, nb,
    pair_ref, mask_ref, sg_ref, sp_ref, sb_ref, so_ref, eg_ref, ep_ref, eb_ref, eo_ref,
    out_ref,
    x_s, q_s, k_s, v_s, g_s, first_s, bias0_s, bias1_s, stage0_s, stage1_s, recv0_s, recv1_s,
    spread_s, fold_s, head_s, send_perm_s, recv_perm_s,
    z_send, z_recv, y_send, y_recv, x_send, x_recv, a_send, a_recv,
):
    nx, ny, nz = dims
    n = nx * ny * nz
    me = lax.axis_index("row")
    x, y, z = me // (ny * nz), (me // nz) % ny, me % nz
    width = x_s.shape[2]
    size = width // HEADS
    blk = nb * ROWS
    tall = blk * HEADS

    barrier = pltpu.get_barrier_semaphore()

    def greet(s, c):
        pl.semaphore_signal(
            barrier, inc=1, device_id={"row": lax.rem(me + s, n)}, device_id_type=MESH
        )
        return c

    lax.fori_loop(1, n, greet, 0)

    def chunk(ref, first, count):
        return ref.at[pl.ds(pl.multiple_of(first * CH, CH), count * CH)]

    def remote(src, dst, send, recv, peer):
        return pltpu.make_async_remote_copy(
            src_ref=src, dst_ref=dst, send_sem=send, recv_sem=recv,
            device_id={"row": peer}, device_id_type=MESH,
        )

    def wait_bytes(ref, count, sem):
        view = ref.at[pl.ds(0, count * CH)]
        pltpu.make_async_copy(view, view, sem).wait()

    spread_s[...] = (iota((tall, blk), 0) // HEADS == iota((tall, blk), 1)).astype(F32).astype(BF16)
    fold_s[...] = (iota((blk, tall), 1) // HEADS == iota((blk, tall), 0)).astype(F32).astype(BF16)
    head_s[...] = (iota((tall, width), 0) % HEADS == iota((tall, width), 1) // size).astype(F32)
    o, i = iota((tall, tall), 0), iota((tall, tall), 1)
    send_perm_s[...] = (
        (o % ROWS) * blk + (o // CH) * ROWS + (o // ROWS) % ROWS == i
    ).astype(F32).astype(BF16)
    recv_perm_s[...] = (
        ((o // ROWS) % nb) * CH + (o // blk) * ROWS + o % ROWS == i
    ).astype(F32).astype(BF16)
    mask_term = (mask_ref[...].astype(F32) - 1.0) * (1e9 * LOG2E)
    v_s[:, :, width:] = jnp.ones((ROWS, v_s.shape[1], width), BF16)

    def share_of_bias(b_ref):
        total = None
        for r in range(ROWS):
            row, col = iota((CH, HEADS), 0), iota((CH, HEADS), 1)
            pick = ((row // HEADS == r) & (row % HEADS == col)).astype(F32).astype(BF16)
            term = nt(nt(pick, b_ref[...]).astype(BF16), x_s[r])
            total = term if total is None else total + term
        return (total * LOG2E + mask_term).astype(BF16)

    def gather_z(t, bias):
        def go(s, c):
            peer = me - z + lax.rem(z + s, nz)
            mine = chunk(bias, me, 1)
            remote(mine, mine, z_send.at[t], z_recv.at[t], peer).start()
            return c

        lax.fori_loop(1, nz, go, 0)

    def gather_y(t, bias):
        wait_bytes(bias, nz - 1, z_recv.at[t])

        def go(s, c):
            peer = me + (lax.rem(y + s, ny) - y) * nz
            line = chunk(bias, me - z, nz)
            remote(line, line, y_send.at[t], y_recv.at[t], peer).start()
            return c

        lax.fori_loop(1, ny, go, 0)

    def gather_x(t, bias):
        wait_bytes(bias, (ny - 1) * nz, y_recv.at[t])
        for s in range(1, nx):
            peer = me + (lax.rem(x + s, nx) - x) * (ny * nz)
            plane = chunk(bias, x * (ny * nz), ny * nz)
            remote(plane, plane, x_send.at[t, s], x_recv.at[t, nx - s], peer).start()

    def project(p_ref):
        for r in range(ROWS):
            out = mm(x_s[r], p_ref[...])
            q_s[r] = (out[:, :width] * (LOG2E / math.sqrt(size))).astype(BF16)
            k_s[r] = out[:, width : 2 * width].astype(BF16)
            v_s[r, :, :width] = out[:, 2 * width : 3 * width].astype(BF16)
            gate = out[:, 3 * width :].astype(BF16).astype(F32)
            g_s[r] = jax.nn.sigmoid(gate)

    def attend(t, bias, o_ref, stage, recv, residual):
        per_plane = ny * nz // nb

        def block(p, c):
            step, half = p // per_plane, p % per_plane
            rel = step ^ (step >> 1)
            plane = lax.rem(x + rel, nx)

            @pl.when((half == 0) & (step > 0))
            def _():
                wait_bytes(bias, ny * nz, x_recv.at[t, rel])

            b = plane * per_plane + lax.rem(half + y * per_plane // ny, per_plane)
            rows = pl.ds(pl.multiple_of(b * tall, tall), tall)
            here = pl.ds(pl.multiple_of(b * blk, blk), blk)
            done = []
            for r in range(ROWS):
                q = (mm(spread_s[...], q_s[r, here, :]) * head_s[...]).astype(BF16)
                s = nt(q, k_s[r]) + bias[rows, :].astype(F32)
                e = jnp.exp2(s - jnp.max(s, axis=-1, keepdims=True)).astype(BF16)
                a = mm(e, v_s[r])
                a = (a[:, :width] * (head_s[...] / a[:, width:])).astype(BF16)
                h = (g_s[r, here, :] * mm(fold_s[...], a)).astype(BF16)
                u = mm(h, o_ref[...])
                if residual is not None:
                    u = residual[r, here, :].astype(F32) + u
                u = u.astype(BF16)
                if residual is not None:
                    first_s[r, here, :] = u
                done.append(u)
            stage[rows, :] = mm(send_perm_s[...], jnp.concatenate(done, axis=0)).astype(BF16)

            def send(k, c):
                peer = b * nb + lax.rem(me + k, nb)

                @pl.when(peer != me)
                def _():
                    remote(
                        chunk(stage, peer, 1), chunk(recv, me, 1), a_send.at[t], a_recv.at[t], peer
                    ).start()

                return c

            lax.fori_loop(0, nb, send, 0)
            return c

        lax.fori_loop(0, n // nb, block, 0)
        mine = pl.ds(pl.multiple_of(me * CH, CH), CH)
        recv[mine, :] = stage[mine, :]
        wait_bytes(recv, n - 1, a_recv.at[t])

    def drain(t, bias, stage):
        wait_bytes(bias, nz - 1, z_send.at[t])
        wait_bytes(bias, (ny - 1) * nz, y_send.at[t])
        for s in range(1, nx):
            wait_bytes(bias, ny * nz, x_send.at[t, s])
        wait_bytes(stage, n - 1, a_send.at[t])

    def update(t, g_ref, p_ref, b_ref, o_ref, bias, stage, recv, residual):
        bias[pl.ds(pl.multiple_of(me * CH, CH), CH), :] = share_of_bias(b_ref)
        if t == 0:
            pl.semaphore_wait(barrier, n - 1)
        gather_z(t, bias)
        project(p_ref)
        gather_y(t, bias)
        gather_x(t, bias)
        attend(t, bias, o_ref, stage, recv, residual)

    for r in range(ROWS):
        x_s[r] = ln(pair_ref[r].astype(F32), sg_ref[...])
    update(0, sg_ref, sp_ref, sb_ref, so_ref, bias0_s, stage0_s, recv0_s, pair_ref)

    def norm_block(b, c):
        rows = pl.ds(pl.multiple_of(b * tall, tall), tall)
        here = pl.ds(pl.multiple_of(b * blk, blk), blk)
        normed = ln(mm(recv_perm_s[...], recv0_s[rows, :]), eg_ref[...])
        for u in range(ROWS):
            x_s[u, here, :] = normed[u * blk : (u + 1) * blk]
        return c

    lax.fori_loop(0, n // nb, norm_block, 0)
    update(1, eg_ref, ep_ref, eb_ref, eo_ref, bias1_s, stage1_s, recv1_s, None)

    def last_block(b, c):
        rows = pl.ds(pl.multiple_of(b * tall, tall), tall)
        here = pl.ds(pl.multiple_of(b * blk, blk), blk)
        late = mm(recv_perm_s[...], recv1_s[rows, :])
        for u in range(ROWS):
            out_ref[u, here, :] = (
                first_s[u, here, :].astype(F32) + late[u * blk : (u + 1) * blk]
            ).astype(BF16)
        return c

    lax.fori_loop(0, n // nb, last_block, 0)
    drain(0, bias0_s, stage0_s)
    drain(1, bias1_s, stage1_s)


def dims_of(n):
    return (4, 4, 8) if n == 128 else (2, 2, n // 4)


def solution(mesh):
    n = mesh.shape["row"]
    dims = dims_of(n)
    nb = min(16, dims[1] * dims[2] // 2)

    def body(pair, token_mask, sg, sp, sb, so, eg, ep, eb, eo):
        rows, count, width = pair.shape
        tall, blk = nb * CH, nb * ROWS
        vmem = pl.BlockSpec(memory_space=pltpu.VMEM)
        dma = pltpu.SemaphoreType.DMA
        return pl.pallas_call(
            functools.partial(kernel, dims, nb),
            out_shape=jax.ShapeDtypeStruct(pair.shape, BF16),
            in_specs=[vmem] * 10,
            out_specs=vmem,
            scratch_shapes=[
                pltpu.VMEM((rows, count, width), BF16),
                pltpu.VMEM((rows, count, width), BF16),
                pltpu.VMEM((rows, count, width), BF16),
                pltpu.VMEM((rows, count, 2 * width), BF16),
                pltpu.VMEM((rows, count, width), F32),
                pltpu.VMEM((rows, count, width), BF16),
                pltpu.VMEM((n * CH, count), BF16),
                pltpu.VMEM((n * CH, count), BF16),
                pltpu.VMEM((n * CH, width), BF16),
                pltpu.VMEM((n * CH, width), BF16),
                pltpu.VMEM((n * CH, width), BF16),
                pltpu.VMEM((n * CH, width), BF16),
                pltpu.VMEM((tall, blk), BF16),
                pltpu.VMEM((blk, tall), BF16),
                pltpu.VMEM((tall, width), F32),
                pltpu.VMEM((tall, tall), BF16),
                pltpu.VMEM((tall, tall), BF16),
                dma((2,)), dma((2,)), dma((2,)), dma((2,)),
                dma((2, dims[0])), dma((2, dims[0])), dma((2,)), dma((2,)),
            ],
            compiler_params=pltpu.CompilerParams(
                collective_id=0, has_side_effects=True, vmem_limit_bytes=56 * 1024 * 1024
            ),
        )(
            pair, token_mask.reshape(1, count), sg.reshape(1, width), sp, sb, so,
            eg.reshape(1, width), ep, eb, eo,
        )

    return jax.shard_map(
        body,
        mesh=mesh,
        in_specs=(P(("rep", "row"), None, None), P("rep"), P(), P(), P(), P(), P(), P(), P(), P()),
        out_specs=P(("rep", "row"), None, None),
        check_vma=False,
    )
```

time: 1570 us -> 165 us (0.11)
  waiting for transfers between devices: 1260 us -> 0 us
  Pallas kernels: 0 us -> 161 us
  blocking collectives: 152 us -> 0 us
  matrix products: 73.5 us -> 0 us
  local copies, waits for them, and re-layouts: 41.3 us -> 4.01 us
  other arithmetic: 16.4 us -> 0 us
    all_gather x2 -> x0, waiting for transfers between devices: 1260 us -> none  [the longest x1 633 us: body(): whole_start = lax.all_gather(bias_rows, 'row', axis=1, tiled=True)]
    pallas_call x0 -> x1, Pallas kernels: none -> 161 us  [body(): pl.pallas_call(functools.partial(kernel, dims, nb), out_shape=jax.ShapeDt...]
    all_to_all x2 -> x0, blocking collectives: 152 us -> none  [the longest x1 75.9 us: body(): lax.all_to_all(jnp.swapaxes(late, 0, 1), 'row', split_axis=0, concat_axis...]
    dot_general x14 -> x0, matrix products: 37.1 us -> none  [the longest x8 25.4 us: attend_block(): jnp.einsum('rhjk,rkhd->rjhd', probs, values, preferred_element_type=jnp.f...]
    sub x8 -> x0, matrix products: 36.4 us -> none  [attend_block(): scores = scores - jnp.max(scores, axis=-1, keepdims=True)]
    dynamic_slice x24 -> x0, local copies, waits for them, and re-layouts: 15.7 us -> none  [the longest x8 5 us: attend_all(): lax.map(one_block, jnp.arange(total // block, dtype=jnp.int32) * block)]
  transfers between devices with their start and end apart: 2 -> 0, of which waited for: 2 -> 0; matrix products, arithmetic and copies ran while one was open for 1% -> 0% of each run, Pallas kernels for 0% -> 0%
where the time goes in v1:
time: 165 us
  Pallas kernels  161 us (98%)
  local copies, waits for them, and re-layouts  4.01 us (2%)
    pallas_call x1, Pallas kernels, body(): pl.pallas_call(functools.partial(kernel, dims, nb), out_shape=jax.ShapeDt...  161 us
    unnamed x7, local copies, waits for them, and re-layouts  4.01 us

profile of v1, /device:TPU:56, one launch (start us, length us, event | category | flops | bytes accessed | tf_op | source)
XLA Modules:
  0.0 164.8 jit_solution(11759935129298086440)
XLA Ops:
  0.0 0.0 copy-start
  0.0 0.7 copy-done
  0.7 0.0 copy-start.1
  0.7 0.7 copy.11.sb_ref
  1.4 0.0 copy-done.1
  1.4 0.7 copy.12.eb_ref
  2.1 160.8 %shard_map.100 = bf16[4,512,128]{2,1,0:T(8,128)(2,1)} custom-call(bf16[4,512,128]{2,1,0:T(8,128)(2,1)} %pair_ref.1, s32[1,512]{1,0:T(1,128)} %bitcast.3, f32[1,128]{1,0:T(1,128)} %bitcast.4, bf16[128,512]{1,0:T(8,128)(2,1)} %sp_ref.1, bf16[128,4]{1,0:T(8,128)(2,1)} %copy.11.sb_ref, bf16[128,128]{1,0:T(8,128)(2,1)} %so_ref.1, f32[1,128]{1,0:T(1,128)} %bitcast.5, ...), custom_call_target="tpu_custom_call" | custom-call | tf_op jit(solution)/shard_map/pallas_call | solution.py:248
  162.9 1.9 %copy.14 = bf16[4,512,128]{2,1,0:T(8,128)(2,1)} copy(bf16[4,512,128]{2,1,0:T(8,128)(2,1)} %shard_map.100) | data formatting | bytes 1048576
Async XLA Ops:
  0.0 0.7 copy-start
  0.7 0.7 copy-start.1

commit v2 on v0

v2 whole, which is shorter than its diff:
```python
import functools
import math

import jax
import jax.numpy as jnp
from jax import lax
from jax.experimental import pallas as pl
from jax.experimental.pallas import tpu as pltpu
from jax.sharding import PartitionSpec as P

MESH = pl.DeviceIdType.MESH
LOG2E = 1.4426950408889634
F32 = jnp.float32
BF16 = jnp.bfloat16
ROWS = 4
TEAM = 2 * ROWS
HEADS = 4
CH = ROWS * HEADS


def iota(shape, dim):
    return lax.broadcasted_iota(jnp.int32, shape, dim)


def one_hot(cond):
    return cond.astype(F32).astype(BF16)


def nt(a, b):
    return lax.dot_general(a, b, (((1,), (1,)), ((), ())), preferred_element_type=F32)


def mm(a, b):
    return jnp.dot(a, b, preferred_element_type=F32)


def ln(wide, gain):
    center = wide - jnp.mean(wide, axis=-1, keepdims=True)
    spread = jnp.mean(center * center, axis=-1, keepdims=True)
    return (center * lax.rsqrt(spread + 1e-05) * gain).astype(BF16)


def kernel(
    dims,
    pair_ref, mask_ref, sg_ref, sp_ref, sb_ref, so_ref, eg_ref, ep_ref, eb_ref, eo_ref,
    out_ref,
    raw0_s, raw1_s, x_s, v_s, score_s, gate_s, res_s, e_s, top_s, low_s, turn_s,
    bias0_s, bias1_s, stage0_s, stage1_s, recv0_s, recv1_s, pick_s, spread_s, wkv_s, wqg_s,
    t_send, t_recv, y_send, y_recv, z_send, z_recv, x_send, x_recv, a_send, a_recv,
):
    nx, ny, nz = dims
    nzi = nz // 2
    per = ny * nzi
    members = nx * per
    me = lax.axis_index("row")
    cls, mine = me % 2, me // 2
    x, y, zi = mine // per, (mine // nzi) % ny, mine % nzi
    width = x_s.shape[2]
    count = x_s.shape[1]
    size = width // HEADS
    quer = per * ROWS
    tall = quer * HEADS
    span = per * TEAM

    barrier = pltpu.get_barrier_semaphore()

    def greet_one(peer):
        pl.semaphore_signal(barrier, inc=1, device_id={"row": peer}, device_id_type=MESH)

    def member(m):
        return 2 * m + cls

    partner = me + 1 - 2 * cls
    greet_one(partner)

    def greet(s, c):
        greet_one(member(lax.rem(mine + s, members)))
        return c

    lax.fori_loop(1, members, greet, 0)

    def remote(src, dst, send, recv, peer):
        return pltpu.make_async_remote_copy(
            src_ref=src, dst_ref=dst, send_sem=send, recv_sem=recv,
            device_id={"row": peer}, device_id_type=MESH,
        )

    def wait_for(view, sem):
        pltpu.make_async_copy(view, view, sem).wait()

    row, col = iota((quer, span), 0), iota((quer, span), 1)
    pick_s[...] = one_hot((row // ROWS) * TEAM + ROWS * cls + row % ROWS == col)
    spread_s[...] = one_hot(iota((tall, quer), 0) // HEADS == iota((tall, quer), 1))
    lane_head = iota((quer, width), 1) // size
    head = (iota((tall, width), 0) % HEADS == iota((tall, width), 1) // size).astype(F32)
    mask_term = (mask_ref[...].astype(F32) - 1.0) * (1e9 * LOG2E)
    v_s[:, :, width:] = jnp.ones((TEAM, count, width), BF16)

    own = ROWS * cls
    other = ROWS - own

    def update(t, g_ref, p_ref, b_ref, o_ref, raw, bias, stage, recv, rounded):
        own_rows = raw.at[pl.ds(own, ROWS)]
        remote(own_rows, own_rows, t_send.at[t], t_recv.at[t], partner).start()

        total = None
        for r in range(ROWS):
            normed = ln(raw[own + r].astype(F32), g_ref[...])
            x_s[own + r] = normed
            a, b = iota((CH, HEADS), 0), iota((CH, HEADS), 1)
            pick = one_hot((a // HEADS == r) & (a % HEADS == b))
            term = nt(mm(pick, b_ref[...]).astype(BF16), normed)
            total = term if total is None else total + term
        bias[x, y, zi] = (total * LOG2E + mask_term).astype(BF16)

        def send_y(s, c):
            peer = member(mine + (lax.rem(y + s, ny) - y) * nzi)
            share = bias.at[x, y, zi]
            remote(share, share, y_send.at[t], y_recv.at[t], peer).start()
            return c

        lax.fori_loop(1, ny, send_y, 0)

        wkv_s[...] = p_ref[:, width : 3 * width]
        wqg_s[:, :width] = p_ref[:, :width]
        wqg_s[:, width:] = p_ref[:, 3 * width :]

        def project(i, c):
            normed = x_s[i]
            kv = mm(normed, wkv_s[...])
            keys = kv[:, :width].astype(BF16)
            v_s[i, :, :width] = kv[:, width:].astype(BF16)
            for p in range(nx):
                part = slice(p * span, (p + 1) * span)
                here = slice(p * quer, (p + 1) * quer)
                both = jnp.concatenate([normed[part], raw[i, part, :]], axis=1)
                both = mm(pick_s[...], both)
                res_s[i, here, :] = both[:, width:]
                qg = mm(both[:, :width].astype(BF16), wqg_s[...])
                gate_s[i, here, :] = jax.nn.sigmoid(qg[:, width:].astype(BF16).astype(F32))
                q = (qg[:, :width] * (LOG2E / math.sqrt(size))).astype(BF16)
                q = (mm(spread_s[...], q) * head).astype(BF16)
                score_s[i, p] = nt(q, keys)
            return c

        lax.fori_loop(own, own + 2, project, 0)

        if ny > 1:
            wait_for(bias.at[0, pl.ds(0, ny - 1), 0], y_recv.at[t])

        def send_z(s, c):
            peer = member(mine + lax.rem(zi + s, nzi) - zi)
            line = bias.at[x, :, zi]
            remote(line, line, z_send.at[t], z_recv.at[t], peer).start()
            return c

        lax.fori_loop(1, nzi, send_z, 0)
        lax.fori_loop(own + 2, own + ROWS, project, 0)
        wait_for(bias.at[0, :, pl.ds(0, nzi - 1)], z_recv.at[t])

        up, down = lax.rem(x + 1, nx), lax.rem(x + nx - 1, nx)
        far = lax.rem(x + 2, nx)
        to_up = member(mine + (up - x) * per)
        to_down = member(mine + (down - x) * per)
        remote(bias.at[x], bias.at[x], x_send.at[t], x_recv.at[t, 1], to_up).start()
        remote(bias.at[x], bias.at[x], x_send.at[t], x_recv.at[t, 0], to_down).start()

        def relay(i, p, peer):
            part = bias.at[p, :, pl.ds(i * (nzi // 2), nzi // 2)]
            remote(part, part, x_send.at[t], x_recv.at[t, 2 + i], peer).start()

        wait_for(raw.at[pl.ds(other, ROWS)], t_recv.at[t])

        def finish(i, c):
            x_s[i] = ln(raw[i].astype(F32), g_ref[...])
            return project(i, c)

        lax.fori_loop(other, other + ROWS, finish, 0)

        def block(step, c):
            @pl.when(step == 1)
            def _():
                wait_for(bias.at[up], x_recv.at[t, 0])
                relay(0, up, to_down)
                wait_for(bias.at[down], x_recv.at[t, 1])
                relay(1, down, to_up)

            @pl.when(step == 3)
            def _():
                for i in range(2):
                    wait_for(bias.at[far, :, pl.ds(i * (nzi // 2), nzi // 2)], x_recv.at[t, 2 + i])

            p = lax.rem(x + (step ^ (step >> 1)), nx)
            here = pl.ds(pl.multiple_of(p * quer, quer), quer)
            for r in range(TEAM):
                for k in range(per):
                    part = slice(k * CH, (k + 1) * CH)
                    s = score_s[r, p, part, :] + bias[p, k // nzi, k % nzi].astype(F32)
                    e_s[r, part, :] = jnp.exp2(s - jnp.max(s, axis=-1, keepdims=True)).astype(BF16)
                out = mm(e_s[r], v_s[r])
                top_s[r] = out[:, :width]
                low_s[r] = out[:, width:]
                top = top_s[r, pl.ds(0, quer, stride=HEADS), :]
                low = low_s[r, pl.ds(0, quer, stride=HEADS), :]
                for h in range(1, HEADS):
                    is_head = lane_head == h
                    rows = pl.ds(h, quer, stride=HEADS)
                    top = jnp.where(is_head, top_s[r, rows, :], top)
                    low = jnp.where(is_head, low_s[r, rows, :], low)
                hid = (gate_s[r, here, :] * (top / low)).astype(BF16)
                u = mm(hid, o_ref[...])
                if rounded:
                    u = u.astype(BF16).astype(F32)
                turn_s[pl.ds(r, quer, stride=TEAM), :] = res_s[r, here, :] + u
            stage[pl.ds(p * per, per)] = turn_s[...].astype(BF16).reshape(per, ROWS * TEAM, width)

            def send(k, c):
                m = p * per + lax.rem(mine + k, per)

                @pl.when(m != mine)
                def _():
                    remote(
                        stage.at[m], recv.at[mine], a_send.at[t], a_recv.at[t], member(m)
                    ).start()

                return c

            lax.fori_loop(0, per, send, 0)
            return c

        lax.fori_loop(0, nx, block, 0)
        recv[mine] = stage[mine]
        wait_for(recv.at[pl.ds(0, members - 1)], a_recv.at[t])

        wait_for(raw.at[pl.ds(own, ROWS)], t_send.at[t])
        if ny > 1:
            wait_for(bias.at[0, pl.ds(0, ny - 1), 0], y_send.at[t])
        wait_for(bias.at[0, :, pl.ds(0, nzi - 1)], z_send.at[t])
        wait_for(bias.at[pl.ds(0, 3)], x_send.at[t])
        wait_for(stage.at[pl.ds(0, members - 1)], a_send.at[t])

    def turned(recv, r):
        part = recv[...].astype(F32).reshape(members, ROWS, TEAM, width)[:, r]
        return part.reshape(members * TEAM, width).astype(BF16)

    for r in range(ROWS):
        raw0_s[own + r] = pair_ref[r]
    pl.semaphore_wait(barrier, members)
    update(0, sg_ref, sp_ref, sb_ref, so_ref, raw0_s, bias0_s, stage0_s, recv0_s, False)
    for r in range(ROWS):
        raw1_s[own + r] = turned(recv0_s, r)
    update(1, eg_ref, ep_ref, eb_ref, eo_ref, raw1_s, bias1_s, stage1_s, recv1_s, True)
    for r in range(ROWS):
        out_ref[r] = turned(recv1_s, r)


def solution(mesh):
    n = mesh.shape["row"]
    dims = (4, 4, 8) if n == 128 else (4, n // 16, 4)

    def body(pair, token_mask, sg, sp, sb, so, eg, ep, eb, eo):
        rows, count, width = pair.shape
        nx, ny, nz = dims
        per, members = ny * nz // 2, n // 2
        quer, span = per * ROWS, per * TEAM
        tall = quer * HEADS
        vmem = pl.BlockSpec(memory_space=pltpu.VMEM)
        dma = pltpu.SemaphoreType.DMA
        return pl.pallas_call(
            functools.partial(kernel, dims),
            out_shape=jax.ShapeDtypeStruct(pair.shape, BF16),
            in_specs=[vmem] * 10,
            out_specs=vmem,
            scratch_shapes=[
                pltpu.VMEM((TEAM, count, width), BF16),
                pltpu.VMEM((TEAM, count, width), BF16),
                pltpu.VMEM((TEAM, count, width), BF16),
                pltpu.VMEM((TEAM, count, 2 * width), BF16),
                pltpu.VMEM((TEAM, nx, tall, count), F32),
                pltpu.VMEM((TEAM, nx * quer, width), F32),
                pltpu.VMEM((TEAM, nx * quer, width), F32),
                pltpu.VMEM((TEAM, tall, count), BF16),
                pltpu.VMEM((TEAM, tall, width), F32),
                pltpu.VMEM((TEAM, tall, width), F32),
                pltpu.VMEM((quer * TEAM, width), F32),
                pltpu.VMEM((nx, ny, nz // 2, CH, count), BF16),
                pltpu.VMEM((nx, ny, nz // 2, CH, count), BF16),
                pltpu.VMEM((members, ROWS * TEAM, width), BF16),
                pltpu.VMEM((members, ROWS * TEAM, width), BF16),
                pltpu.VMEM((members, ROWS * TEAM, width), BF16),
                pltpu.VMEM((members, ROWS * TEAM, width), BF16),
                pltpu.VMEM((quer, span), BF16),
                pltpu.VMEM((tall, quer), BF16),
                pltpu.VMEM((width, 2 * width), BF16),
                pltpu.VMEM((width, 2 * width), BF16),
                dma((2,)), dma((2,)), dma((2,)), dma((2,)), dma((2,)), dma((2,)),
                dma((2,)), dma((2, 4)), dma((2,)), dma((2,)),
            ],
            compiler_params=pltpu.CompilerParams(
                collective_id=0, has_side_effects=True, vmem_limit_bytes=60 * 1024 * 1024
            ),
        )(
            pair, token_mask.reshape(1, count), sg.reshape(1, width), sp, sb.T, so,
            eg.reshape(1, width), ep, eb.T, eo,
        )

    return jax.shard_map(
        body,
        mesh=mesh,
        in_specs=(P(("rep", "row"), None, None), P("rep"), P(), P(), P(), P(), P(), P(), P(), P()),
        out_specs=P(("rep", "row"), None, None),
        check_vma=False,
    )
```

time: 1570 us -> 111 us (0.07)
  waiting for transfers between devices: 1260 us -> 0 us
  blocking collectives: 152 us -> 0 us
  Pallas kernels: 0 us -> 108 us
  matrix products: 73.5 us -> 0 us
  local copies, waits for them, and re-layouts: 41.3 us -> 1.87 us
  other arithmetic: 16.4 us -> 0 us
    all_gather x2 -> x0, waiting for transfers between devices: 1260 us -> none  [the longest x1 633 us: body(): whole_start = lax.all_gather(bias_rows, 'row', axis=1, tiled=True)]
    all_to_all x2 -> x0, blocking collectives: 152 us -> none  [the longest x1 75.9 us: body(): lax.all_to_all(jnp.swapaxes(late, 0, 1), 'row', split_axis=0, concat_axis...]
    pallas_call x0 -> x1, Pallas kernels: none -> 108 us  [body(): pl.pallas_call(functools.partial(kernel, dims), out_shape=jax.ShapeDtypeS...]
    dot_general x14 -> x0, matrix products: 37.1 us -> none  [the longest x8 25.4 us: attend_block(): jnp.einsum('rhjk,rkhd->rjhd', probs, values, preferred_element_type=jnp.f...]
    sub x8 -> x0, matrix products: 36.4 us -> none  [attend_block(): scores = scores - jnp.max(scores, axis=-1, keepdims=True)]
    dynamic_slice x24 -> x0, local copies, waits for them, and re-layouts: 15.7 us -> none  [the longest x8 5 us: attend_all(): lax.map(one_block, jnp.arange(total // block, dtype=jnp.int32) * block)]
  transfers between devices with their start and end apart: 2 -> 0, of which waited for: 2 -> 0; matrix products, arithmetic and copies ran while one was open for 1% -> 0% of each run, Pallas kernels for 0% -> 0%
where the time goes in v2:
time: 111 us; the launch traced here: 110 us
  Pallas kernels  108 us (97%)
  local copies, waits for them, and re-layouts  1.87 us (2%)
    pallas_call x1, Pallas kernels, body(): pl.pallas_call(functools.partial(kernel, dims), out_shape=jax.ShapeDtypeS...  108 us

profile of v2, /device:TPU:56, one launch (start us, length us, event | category | flops | bytes accessed | tf_op | source)
XLA Modules:
  0.0 109.8 jit_solution(943461604907490400)
XLA Ops:
  0.0 108.0 %shard_map.100 = bf16[4,512,128]{2,1,0:T(8,128)(2,1)} custom-call(bf16[4,512,128]{2,1,0:T(8,128)(2,1)} %pair_ref.1, s32[1,512]{1,0:T(1,128)} %bitcast.5, f32[1,128]{1,0:T(1,128)} %bitcast.8, bf16[128,512]{1,0:T(8,128)(2,1)} %sp_ref.1, bf16[4,128]{1,0:T(4,128)(2,1)} %bitcast.6, bf16[128,128]{1,0:T(8,128)(2,1)} %so_ref.1, f32[1,128]{1,0:T(1,128)} %bitcast.9, ...), custom_call_target="tpu_custom_call" | custom-call | tf_op jit(solution)/shard_map/pallas_call | solution.py:269
  108.0 1.9 %copy.12 = bf16[4,512,128]{2,1,0:T(8,128)(2,1)} copy(bf16[4,512,128]{2,1,0:T(8,128)(2,1)} %shard_map.100) | data formatting | bytes 1048576

commit v3 on v2

v3 whole, which is shorter than its diff:
```python
import functools
import math

import jax
import jax.numpy as jnp
from jax import lax
from jax.experimental import pallas as pl
from jax.experimental.pallas import tpu as pltpu
from jax.sharding import PartitionSpec as P

MESH = pl.DeviceIdType.MESH
LOG2E = 1.4426950408889634
F32 = jnp.float32
BF16 = jnp.bfloat16
ROWS = 4
TEAM = 2 * ROWS
HEADS = 4
CH = ROWS * HEADS


def iota(shape, dim):
    return lax.broadcasted_iota(jnp.int32, shape, dim)


def one_hot(cond):
    return cond.astype(F32).astype(BF16)


def nt(a, b):
    return lax.dot_general(a, b, (((1,), (1,)), ((), ())), preferred_element_type=F32)


def mm(a, b):
    return jnp.dot(a, b, preferred_element_type=F32)


def ln(wide, gain):
    center = wide - jnp.mean(wide, axis=-1, keepdims=True)
    spread = jnp.mean(center * center, axis=-1, keepdims=True)
    return (center * lax.rsqrt(spread + 1e-05) * gain).astype(BF16)


def kernel(
    dims,
    pair_ref, mask_ref, sg_ref, sp_ref, sb_ref, so_ref, eg_ref, ep_ref, eb_ref, eo_ref,
    out_ref,
    raw0_s, raw1_s, x_s, v_s, score_s, gate_s, res_s, e_s, top_s, low_s, turn_s,
    bias0_s, bias1_s, stage0_s, stage1_s, recv0_s, recv1_s, pick_s, spread_s, wkv_s, wqg_s,
    t_send, t_recv, y_send, y_recv, z_send, z_recv, x_send, x_recv, a_send, a_recv,
):
    nx, ny, nz = dims
    nyi = ny // 2
    per = nyi * nz
    members = nx * per
    me = lax.axis_index("row")
    x, y, z = me // (ny * nz), (me // nz) % ny, me % nz
    cls, yi = y % 2, y // 2
    mine = (x * nyi + yi) * nz + z
    width = x_s.shape[2]
    count = x_s.shape[1]
    size = width // HEADS
    quer = per * ROWS
    tall = quer * HEADS
    span = per * TEAM
    group = nz * TEAM

    barrier = pltpu.get_barrier_semaphore()

    def greet_one(peer):
        pl.semaphore_signal(barrier, inc=1, device_id={"row": peer}, device_id_type=MESH)

    def member(m):
        return (2 * (m // nz) + cls) * nz + m % nz

    partner = me + nz * (1 - 2 * cls)
    greet_one(partner)

    def greet(s, c):
        greet_one(member(lax.rem(mine + s, members)))
        return c

    lax.fori_loop(1, members, greet, 0)

    def remote(src, dst, send, recv, peer):
        return pltpu.make_async_remote_copy(
            src_ref=src, dst_ref=dst, send_sem=send, recv_sem=recv,
            device_id={"row": peer}, device_id_type=MESH,
        )

    def wait_for(view, sem):
        pltpu.make_async_copy(view, view, sem).wait()

    def given(token):
        rest = token % group
        return token - rest + (rest // ROWS) % 2 * (nz * ROWS) + rest // TEAM * ROWS + rest % ROWS

    spread_s[...] = one_hot(iota((tall, quer), 0) // HEADS == iota((tall, quer), 1))
    lane_head = iota((quer, width), 1) // size
    head = (iota((tall, width), 0) % HEADS == iota((tall, width), 1) // size).astype(F32)
    far_mask = (1e9 * LOG2E)

    own = ROWS * cls
    other = ROWS - own
    up, down, far = lax.rem(x + 1, nx), lax.rem(x + nx - 1, nx), lax.rem(x + 2, nx)
    to_up = member(mine + (up - x) * per)
    to_down = member(mine + (down - x) * per)

    def half(ref, p, i):
        if nz > 1:
            return ref.at[p, :, pl.ds(i * (nz // 2), nz // 2)]
        return ref.at[p, pl.ds(i * (nyi // 2), nyi // 2)]

    def head_rows(b_ref, r):
        a, b = iota((CH, HEADS), 0), iota((CH, HEADS), 1)
        return mm(one_hot((a // HEADS == r) & (a % HEADS == b)), b_ref[...]).astype(BF16)

    def send_y(t, bias):
        def go(s, c):
            peer = member(mine + (lax.rem(yi + s, nyi) - yi) * nz)
            share = bias.at[x, yi, z]
            remote(share, share, y_send.at[t], y_recv.at[t], peer).start()
            return c

        lax.fori_loop(1, nyi, go, 0)

    def update(t, g_ref, p_ref, o_ref, raw, bias, stage, recv, on_last):
        row, col = iota((quer, span), 0), iota((quer, span), 1)
        token = row // ROWS * TEAM + ROWS * cls + row % ROWS
        pick_s[...] = one_hot((given(token) if t == 0 else token) == col)
        wkv_s[...] = p_ref[:, width : 3 * width]
        wqg_s[:, :width] = p_ref[:, :width]
        wqg_s[:, width:] = p_ref[:, 3 * width :]

        def project(i):
            pair = (i, i + 1)
            kv = [mm(x_s[k], wkv_s[...]) for k in pair]
            keys = [a[:, :width].astype(BF16) for a in kv]
            for k, a in zip(pair, kv):
                v_s[k, :, :width] = a[:, width:].astype(BF16)
            for p in range(nx):
                part = slice(p * span, (p + 1) * span)
                here = slice(p * quer, (p + 1) * quer)
                both = jnp.concatenate(
                    [x_s[i, part, :], x_s[i + 1, part, :], raw[i, part, :], raw[i + 1, part, :]],
                    axis=1,
                )
                both = mm(pick_s[...], both)
                normed = both[:, : 2 * width].astype(BF16)
                normed = jnp.concatenate([normed[:, :width], normed[:, width:]], axis=0)
                qg = mm(normed, wqg_s[...])
                gate = jax.nn.sigmoid(qg[:, width:].astype(BF16).astype(F32))
                q = (qg[:, :width] * (LOG2E / math.sqrt(size))).astype(BF16)
                q = mm(spread_s[...], jnp.concatenate([q[:quer], q[quer:]], axis=1))
                for n, k in enumerate(pair):
                    res_s[k, here, :] = both[:, (2 + n) * width : (3 + n) * width]
                    gate_s[k, here, :] = gate[n * quer : (n + 1) * quer]
                    one = (q[:, n * width : (n + 1) * width] * head).astype(BF16)
                    score_s[k, p] = nt(one, keys[n])

        project(own)
        if nyi > 1:
            wait_for(bias.at[0, pl.ds(0, nyi - 1), 0], y_recv.at[t])

        def send_z(s, c):
            peer = member(mine + lax.rem(z + s, nz) - z)
            line = bias.at[x, :, z]
            remote(line, line, z_send.at[t], z_recv.at[t], peer).start()
            return c

        if nz > 1:
            lax.fori_loop(1, nz, send_z, 0)
        project(own + 2)
        if nz > 1:
            wait_for(bias.at[0, :, pl.ds(0, nz - 1)], z_recv.at[t])

        for i in range(2):
            for sem, peer, h in ((0, to_down, i), (2, to_up, 1 - i)):
                part = half(bias, x, h)
                remote(part, part, x_send.at[t], x_recv.at[t, sem + h], peer).start()

        wait_for(raw.at[pl.ds(other, ROWS)], t_recv.at[t])
        for r in range(2):
            x_s[other + r] = ln(raw[other + r].astype(F32), g_ref[...])
        project(other)

        wait_for(half(bias, up, 0), x_recv.at[t, 0])
        part = half(bias, up, 0)
        remote(part, part, x_send.at[t], x_recv.at[t, 4], to_down).start()
        wait_for(half(bias, down, 1), x_recv.at[t, 3])
        part = half(bias, down, 1)
        remote(part, part, x_send.at[t], x_recv.at[t, 5], to_up).start()

        for r in range(2, ROWS):
            x_s[other + r] = ln(raw[other + r].astype(F32), g_ref[...])
        project(other + 2)

        def block(step, c):
            @pl.when(step == 1)
            def _():
                wait_for(half(bias, up, 1), x_recv.at[t, 1])

            @pl.when(step == 2)
            def _():
                wait_for(half(bias, down, 0), x_recv.at[t, 2])

            @pl.when(step == 3)
            def _():
                on_last()
                wait_for(half(bias, far, 0), x_recv.at[t, 4])
                wait_for(half(bias, far, 1), x_recv.at[t, 5])

            p = lax.rem(x + (step ^ (step >> 1)), nx)
            here = pl.ds(pl.multiple_of(p * quer, quer), quer)
            for r in range(TEAM):
                for k in range(per):
                    part = slice(k * CH, (k + 1) * CH)
                    s = score_s[r, p, part, :] + bias[p, k // nz, k % nz].astype(F32)
                    e_s[r, part, :] = jnp.exp2(s - jnp.max(s, axis=-1, keepdims=True)).astype(BF16)
                out = mm(e_s[r], v_s[r])
                top_s[r] = out[:, :width]
                low_s[r] = out[:, width:]
            hid = []
            for r in range(TEAM):
                top = top_s[r, pl.ds(0, quer, stride=HEADS), :]
                low = low_s[r, pl.ds(0, quer, stride=HEADS), :]
                for h in range(1, HEADS):
                    rows = pl.ds(h, quer, stride=HEADS)
                    top = jnp.where(lane_head == h, top_s[r, rows, :], top)
                    low = jnp.where(lane_head == h, low_s[r, rows, :], low)
                hid.append((gate_s[r, here, :] * (top / low)).astype(BF16))
            u = mm(jnp.concatenate(hid, axis=0), o_ref[...])
            if t == 1:
                u = u.astype(BF16).astype(F32)
            for r in range(TEAM):
                turn_s[pl.ds(r, quer, stride=TEAM), :] = (
                    res_s[r, here, :] + u[r * quer : (r + 1) * quer]
                )
            stage[pl.ds(p * per, per)] = turn_s[...].astype(BF16).reshape(per, ROWS * TEAM, width)

            def send(k, c):
                m = p * per + lax.rem(mine + k, per)

                @pl.when(m != mine)
                def _():
                    remote(
                        stage.at[m], recv.at[mine], a_send.at[t], a_recv.at[t, step], member(m)
                    ).start()

                return c

            lax.fori_loop(0, per, send, 0)

            @pl.when(step == 0)
            def _():
                recv[mine] = stage[mine]

            return c

        lax.fori_loop(0, nx, block, 0)

    def taken(t, recv, n):
        p = (x, down, up, far)[n]
        wait_for(recv.at[pl.ds(0, per - (n == 0))], a_recv.at[t, n])
        part = recv[pl.ds(p * per, per)].astype(F32)
        return p, part.reshape(per, ROWS, TEAM, width)

    def arrive(n):
        p, part = taken(0, recv0_s, n)
        here = pl.ds(pl.multiple_of(p * span, span), span)
        total = None
        for r in range(ROWS):
            row = part[:, r].reshape(span, width)
            raw1_s[own + r, here, :] = row.astype(BF16)
            normed = ln(row, eg_ref[...])
            x_s[own + r, here, :] = normed
            term = nt(head_rows(eb_ref, r), normed)
            total = term if total is None else total + term
        piece = raw1_s.at[pl.ds(own, ROWS), here, :]
        remote(piece, piece, t_send.at[1], t_recv.at[1], partner).start()
        order = given(p * span + iota((count, span), 1))
        order = one_hot(iota((count, span), 0) == order)
        mask = mm(jnp.broadcast_to(mask_ref[...].astype(F32).astype(BF16), (CH, count)), order)
        bias1_s[x, yi, z, :, here] = (total * LOG2E + (mask - 1.0) * far_mask).astype(BF16)

    def drain(t, raw, bias, stage):
        wait_for(raw.at[pl.ds(own, ROWS)], t_send.at[t])
        if nyi > 1:
            wait_for(bias.at[0, pl.ds(0, nyi - 1), 0], y_send.at[t])
        if nz > 1:
            wait_for(bias.at[0, :, pl.ds(0, nz - 1)], z_send.at[t])
        wait_for(bias.at[pl.ds(0, 3)], x_send.at[t])
        wait_for(stage.at[pl.ds(0, members - 1)], a_send.at[t])

    for r in range(ROWS):
        raw0_s[own + r] = pair_ref[r]
    v_s[:, :, width:] = jnp.ones((TEAM, count, width), BF16)
    total = None
    for r in range(ROWS):
        normed = ln(pair_ref[r].astype(F32), sg_ref[...])
        x_s[own + r] = normed
        term = nt(head_rows(sb_ref, r), normed)
        total = term if total is None else total + term
    mask = mask_ref[...].astype(F32)
    bias0_s[x, yi, z] = (total * LOG2E + (mask - 1.0) * far_mask).astype(BF16)
    pl.semaphore_wait(barrier, members)
    send_y(0, bias0_s)
    rows = raw0_s.at[pl.ds(own, ROWS)]
    remote(rows, rows, t_send.at[0], t_recv.at[0], partner).start()

    def early():
        arrive(0)
        arrive(1)

    update(0, sg_ref, sp_ref, so_ref, raw0_s, bias0_s, stage0_s, recv0_s, early)
    arrive(2)
    arrive(3)
    send_y(1, bias1_s)
    update(1, eg_ref, ep_ref, eo_ref, raw1_s, bias1_s, stage1_s, recv1_s, lambda: None)
    order = one_hot(iota((span, span), 0) == given(iota((span, span), 1)))
    for n in range(nx):
        p, part = taken(1, recv1_s, n)
        here = pl.ds(pl.multiple_of(p * span, span), span)
        part = jnp.concatenate([part[:, r].reshape(span, width) for r in range(ROWS)], axis=1)
        part = mm(order, part.astype(BF16)).astype(BF16)
        for r in range(ROWS):
            out_ref[r, here, :] = part[:, r * width : (r + 1) * width]
    drain(0, raw0_s, bias0_s, stage0_s)
    drain(1, raw1_s, bias1_s, stage1_s)


def solution(mesh):
    n = mesh.shape["row"]
    dims = (4, 4, 8) if n == 128 else (4, 4, 1) if n == 16 else (4, 2, 2)

    def body(pair, token_mask, sg, sp, sb, so, eg, ep, eb, eo):
        rows, count, width = pair.shape
        nx, ny, nz = dims
        per, members = ny * nz // 2, n // 2
        quer, span = per * ROWS, per * TEAM
        tall = quer * HEADS
        vmem = pl.BlockSpec(memory_space=pltpu.VMEM)
        dma = pltpu.SemaphoreType.DMA
        return pl.pallas_call(
            functools.partial(kernel, dims),
            out_shape=jax.ShapeDtypeStruct(pair.shape, BF16),
            in_specs=[vmem] * 10,
            out_specs=vmem,
            scratch_shapes=[
                pltpu.VMEM((TEAM, count, width), BF16),
                pltpu.VMEM((TEAM, count, width), BF16),
                pltpu.VMEM((TEAM, count, width), BF16),
                pltpu.VMEM((TEAM, count, 2 * width), BF16),
                pltpu.VMEM((TEAM, nx, tall, count), F32),
                pltpu.VMEM((TEAM, nx * quer, width), F32),
                pltpu.VMEM((TEAM, nx * quer, width), F32),
                pltpu.VMEM((TEAM, tall, count), BF16),
                pltpu.VMEM((TEAM, tall, width), F32),
                pltpu.VMEM((TEAM, tall, width), F32),
                pltpu.VMEM((quer * TEAM, width), F32),
                pltpu.VMEM((nx, ny // 2, nz, CH, count), BF16),
                pltpu.VMEM((nx, ny // 2, nz, CH, count), BF16),
                pltpu.VMEM((members, ROWS * TEAM, width), BF16),
                pltpu.VMEM((members, ROWS * TEAM, width), BF16),
                pltpu.VMEM((members, ROWS * TEAM, width), BF16),
                pltpu.VMEM((members, ROWS * TEAM, width), BF16),
                pltpu.VMEM((quer, span), BF16),
                pltpu.VMEM((tall, quer), BF16),
                pltpu.VMEM((width, 2 * width), BF16),
                pltpu.VMEM((width, 2 * width), BF16),
                dma((2,)), dma((2,)), dma((2,)), dma((2,)), dma((2,)), dma((2,)),
                dma((2,)), dma((2, 6)), dma((2,)), dma((2, 4)),
            ],
            compiler_params=pltpu.CompilerParams(
                collective_id=0, has_side_effects=True, vmem_limit_bytes=60 * 1024 * 1024
            ),
        )(
            pair, token_mask.reshape(1, count), sg.reshape(1, width), sp, sb.T, so,
            eg.reshape(1, width), ep, eb.T, eo,
        )

    return jax.shard_map(
        body,
        mesh=mesh,
        in_specs=(P(("rep", "row"), None, None), P("rep"), P(), P(), P(), P(), P(), P(), P(), P()),
        out_specs=P(("rep", "row"), None, None),
        check_vma=False,
    )
```

time: 111 us -> 93.3 us (0.84)
  Pallas kernels: 108 us -> 91.3 us
    pallas_call x1, Pallas kernels: 108 us -> 91.3 us  [body(): pl.pallas_call(functools.partial(kernel, dims), out_shape=jax.ShapeDtypeS...]
where the time goes in v3:
time: 93.3 us; the launch traced here: 93.1 us
  Pallas kernels  91.3 us (98%)
  local copies, waits for them, and re-layouts  1.87 us (2%)
    pallas_call x1, Pallas kernels, body(): pl.pallas_call(functools.partial(kernel, dims), out_shape=jax.ShapeDtypeS...  91.3 us
    unnamed x1, local copies, waits for them, and re-layouts  1.87 us

profile of v3, /device:TPU:56, one launch (start us, length us, event | category | flops | bytes accessed | tf_op | source)
XLA Modules:
  0.0 93.1 jit_solution(13329739986729333639)
XLA Ops:
  0.0 91.3 %shard_map.100 = bf16[4,512,128]{2,1,0:T(8,128)(2,1)} custom-call(bf16[4,512,128]{2,1,0:T(8,128)(2,1)} %pair_ref.1, s32[1,512]{1,0:T(1,128)} %bitcast.5, f32[1,128]{1,0:T(1,128)} %bitcast.8, bf16[128,512]{1,0:T(8,128)(2,1)} %sp_ref.1, bf16[4,128]{1,0:T(4,128)(2,1)} %bitcast.6, bf16[128,128]{1,0:T(8,128)(2,1)} %so_ref.1, f32[1,128]{1,0:T(1,128)} %bitcast.9, ...), custom_call_target="tpu_custom_call" | custom-call | tf_op jit(solution)/shard_map/pallas_call | solution.py:343
  91.3 1.9 %copy.12 = bf16[4,512,128]{2,1,0:T(8,128)(2,1)} copy(bf16[4,512,128]{2,1,0:T(8,128)(2,1)} %shard_map.100) | data formatting | bytes 1048576

commit v4 on v3

v4 whole, which is shorter than its diff:
```python
import functools
import math

import jax
import jax.numpy as jnp
from jax import lax
from jax.experimental import pallas as pl
from jax.experimental.pallas import tpu as pltpu
from jax.sharding import PartitionSpec as P

MESH = pl.DeviceIdType.MESH
LOG2E = 1.4426950408889634
F32 = jnp.float32
BF16 = jnp.bfloat16
ROWS = 4
TEAM = 2 * ROWS
HEADS = 4
CH = ROWS * HEADS


def iota(shape, dim):
    return lax.broadcasted_iota(jnp.int32, shape, dim)


def one_hot(cond):
    return cond.astype(F32).astype(BF16)


def nt(a, b):
    return lax.dot_general(a, b, (((1,), (1,)), ((), ())), preferred_element_type=F32)


def mm(a, b):
    return jnp.dot(a, b, preferred_element_type=F32)


def ln(wide, gain):
    center = wide - jnp.mean(wide, axis=-1, keepdims=True)
    spread = jnp.mean(center * center, axis=-1, keepdims=True)
    return (center * lax.rsqrt(spread + 1e-05) * gain).astype(BF16)


def kernel(
    dims,
    pair_ref, mask_ref, sg_ref, sp_ref, sb_ref, so_ref, eg_ref, ep_ref, eb_ref, eo_ref,
    out_ref,
    raw0_s, raw1_s, x_s, v_s, score_s, gate_s, res_s, e_s, top_s, low_s, turn_s,
    bias0_s, bias1_s, stage0_s, stage1_s, recv0_s, recv1_s, pick_s, spread_s, wkv_s, wqg_s,
    t_send, t_recv, z_send, z_recv, x_send, x_recv, a_send, a_recv,
):
    nx, ny, nz = dims
    nyi, nzh = ny // 2, nz // 2
    near = nyi * nzh
    per = 2 * near
    members = nx * per
    me = lax.axis_index("row")
    x, y, z = me // (ny * nz), (me // nz) % ny, me % nz
    cls, yi = y % 2, y // 2
    hz, local = z // nzh, yi * nzh + z % nzh
    mine = (x * nyi + yi) * nz + z
    width = x_s.shape[2]
    count = x_s.shape[1]
    size = width // HEADS
    quer = near * ROWS
    tall = quer * HEADS
    span = per * TEAM
    group = nz * TEAM

    barrier = pltpu.get_barrier_semaphore()

    def greet_one(peer):
        pl.semaphore_signal(barrier, inc=1, device_id={"row": peer}, device_id_type=MESH)

    def member(m):
        return (2 * (m // nz) + cls) * nz + m % nz

    def place(p, half, i):
        return (p * nyi + i // nzh) * nz + half * nzh + i % nzh

    partner = me + nz * (1 - 2 * cls)
    greet_one(partner)

    def greet(s, c):
        greet_one(member(lax.rem(mine + s, members)))
        return c

    lax.fori_loop(1, members, greet, 0)

    def remote(src, dst, send, recv, peer):
        return pltpu.make_async_remote_copy(
            src_ref=src, dst_ref=dst, send_sem=send, recv_sem=recv,
            device_id={"row": peer}, device_id_type=MESH,
        )

    def wait_for(view, sem):
        pltpu.make_async_copy(view, view, sem).wait()

    def given(token):
        rest = token % group
        return token - rest + (rest // ROWS) % 2 * (nz * ROWS) + rest // TEAM * ROWS + rest % ROWS

    spread_s[...] = one_hot(iota((tall, quer), 0) // HEADS == iota((tall, quer), 1))
    lane_head = iota((quer, width), 1) // size
    head = (iota((tall, width), 0) % HEADS == iota((tall, width), 1) // size).astype(F32)
    far_mask = 1e9 * LOG2E

    own = ROWS * cls
    other = ROWS - own
    up, down, far = lax.rem(x + 1, nx), lax.rem(x + nx - 1, nx), lax.rem(x + 2, nx)
    to_up = member(mine + (up - x) * per)
    to_down = member(mine + (down - x) * per)

    def part_of(bias, p, late):
        half = (hz + late) % 2
        return bias.at[p, :, pl.ds(half * nzh, nzh)]

    def quarter(bias, p, i, late):
        half = (hz + late) % 2
        return bias.at[p, i, pl.ds(half * nzh, nzh)]

    def head_rows(b_ref, r):
        a, b = iota((CH, HEADS), 0), iota((CH, HEADS), 1)
        return mm(one_hot((a // HEADS == r) & (a % HEADS == b)), b_ref[...]).astype(BF16)

    def gather_plane(t, bias):
        for late in range(2):

            def go(s, c):
                peer = member(place(x, (hz + late) % 2, lax.rem(local + s, near)))
                share = bias.at[x, yi, z]
                remote(share, share, z_send.at[t], z_recv.at[t, late], peer).start()
                return c

            lax.fori_loop(1 - late, near, go, 0)

    def to_neighbours(t, bias, late):
        part = part_of(bias, x, late)
        remote(part, part, x_send.at[t], x_recv.at[t, late], to_down).start()
        remote(part, part, x_send.at[t], x_recv.at[t, 2 + late], to_up).start()

    def relay(t, bias, late):
        wait_for(part_of(bias, up, late), x_recv.at[t, late])
        part = quarter(bias, up, 0, late)
        remote(part, part, x_send.at[t], x_recv.at[t, 4 + late], to_down).start()
        wait_for(part_of(bias, down, late), x_recv.at[t, 2 + late])
        part = quarter(bias, down, 1, late)
        remote(part, part, x_send.at[t], x_recv.at[t, 6 + late], to_up).start()

    def from_far(t, bias, late):
        wait_for(quarter(bias, far, 0, late), x_recv.at[t, 4 + late])
        wait_for(quarter(bias, far, 1, late), x_recv.at[t, 6 + late])

    def update(t, g_ref, p_ref, o_ref, raw, bias, stage, recv, on_last):
        row, col = iota((2 * quer, span), 0), iota((2 * quer, span), 1)
        share = row // ROWS
        token = place(0, share // near, share % near) * TEAM + ROWS * cls + row % ROWS
        pick_s[...] = one_hot((given(token) if t == 0 else token) == col)
        wkv_s[...] = p_ref[:, width : 3 * width]
        wqg_s[:, :width] = p_ref[:, :width]
        wqg_s[:, width:] = p_ref[:, 3 * width :]

        def project(i):
            pair = (i, i + 1)
            kv = [mm(x_s[k], wkv_s[...]) for k in pair]
            keys = [a[:, :width].astype(BF16) for a in kv]
            for k, a in zip(pair, kv):
                v_s[k, :, :width] = a[:, width:].astype(BF16)
            for p in range(nx):
                part = slice(p * span, (p + 1) * span)
                both = jnp.concatenate(
                    [x_s[i, part, :], x_s[i + 1, part, :], raw[i, part, :], raw[i + 1, part, :]],
                    axis=1,
                )
                both = mm(pick_s[...], both)
                normed = both[:, : 2 * width].astype(BF16)
                normed = jnp.concatenate([normed[:, :width], normed[:, width:]], axis=0)
                qg = mm(normed, wqg_s[...])
                gate = jax.nn.sigmoid(qg[:, width:].astype(BF16).astype(F32))
                q = (qg[:, :width] * (LOG2E / math.sqrt(size))).astype(BF16)
                for n, k in enumerate(pair):
                    res_s[k, p] = both[:, (2 + n) * width : (3 + n) * width]
                    gate_s[k, p] = gate[2 * n * quer : 2 * (n + 1) * quer]
                for half in range(2):
                    lo = half * quer
                    two = [q[lo + 2 * n * quer : lo + (2 * n + 1) * quer] for n in range(2)]
                    wide = mm(spread_s[...], jnp.concatenate(two, axis=1))
                    for n, k in enumerate(pair):
                        one = (wide[:, n * width : (n + 1) * width] * head).astype(BF16)
                        score_s[k, p, half] = nt(one, keys[n])

        def finish(i):
            for k in (i, i + 1):
                x_s[k] = ln(raw[k].astype(F32), g_ref[...])
            project(i)

        project(own)
        project(own + 2)
        wait_for(bias.at[0, 0, pl.ds(0, near - 1)], z_recv.at[t, 0])
        to_neighbours(t, bias, 0)
        if t == 0:
            wait_for(raw.at[pl.ds(other, 2)], t_recv.at[0])
        else:
            wait_for(raw.at[pl.ds(other, ROWS)], t_recv.at[2])
        finish(other)
        wait_for(part_of(bias, 0, 0), z_recv.at[t, 1])
        to_neighbours(t, bias, 1)

        def unit(n, c):
            @pl.when(n == 2)
            def _():
                relay(t, bias, 0)

            @pl.when(n == 4)
            def _():
                if t == 0:
                    wait_for(raw.at[pl.ds(other + 2, 2)], t_recv.at[1])
                finish(other + 2)
                relay(t, bias, 1)

            @pl.when(n == 8)
            def _():
                from_far(t, bias, 0)

            @pl.when(n == 14)
            def _():
                on_last()
                from_far(t, bias, 1)

            q = (n - 8) // 2
            rel = jnp.where(n >= 8, jnp.where((q == 0) | (q == 3), 3, q), jnp.maximum(n % 4 - 1, 0))
            late = jnp.where(n >= 8, (q > 0).astype(jnp.int32), (n % 4 == 1).astype(jnp.int32))
            kind = jnp.where(n >= 8, n % 2, n // 4)
            p = lax.rem(x + (rel ^ (rel >> 1)), nx)
            half = (hz + late) % 2
            side = (cls + kind) % 2
            base = ROWS * side
            for r in range(ROWS):
                for k in range(near):
                    part = slice(k * CH, (k + 1) * CH)
                    add = bias[p, k // nzh, half * nzh + k % nzh].astype(F32)
                    s = score_s[base + r, p, half, part, :] + add
                    e_s[r, part, :] = jnp.exp2(s - jnp.max(s, axis=-1, keepdims=True)).astype(BF16)
                out = mm(e_s[r], v_s[base + r])
                top_s[r] = out[:, :width]
                low_s[r] = out[:, width:]
            here = pl.ds(pl.multiple_of(half * quer, quer), quer)
            hid = []
            for r in range(ROWS):
                top = top_s[r, pl.ds(0, quer, stride=HEADS), :]
                low = low_s[r, pl.ds(0, quer, stride=HEADS), :]
                for h in range(1, HEADS):
                    rows = pl.ds(h, quer, stride=HEADS)
                    top = jnp.where(lane_head == h, top_s[r, rows, :], top)
                    low = jnp.where(lane_head == h, low_s[r, rows, :], low)
                hid.append((gate_s[base + r, p, here, :] * (top / low)).astype(BF16))
            u = mm(jnp.concatenate(hid, axis=0), o_ref[...])
            if t == 1:
                u = u.astype(BF16).astype(F32)
            for r in range(ROWS):
                turn_s[pl.ds(r, quer, stride=ROWS), :] = (
                    res_s[base + r, p, here, :] + u[r * quer : (r + 1) * quer]
                )
            turned = turn_s[...].astype(BF16).reshape(near, CH, width)
            for i in range(nyi):
                stage[pl.ds(place(p, half, i * nzh), nzh), side] = turned[i * nzh : (i + 1) * nzh]

            def send(k, c):
                m = place(p, half, lax.rem(local + k, near))

                @pl.when(m != mine)
                def _():
                    remote(
                        stage.at[m, side], recv.at[mine, side], a_send.at[t], a_recv.at[t, rel],
                        member(m),
                    ).start()

                return c

            lax.fori_loop(0, near, send, 0)

            @pl.when((n == 0) | (n == 4))
            def _():
                recv[mine, side] = stage[mine, side]

            return c

        lax.fori_loop(0, 16, unit, 0)

    def taken(t, recv, n):
        p = (x, down, up, far)[n]
        wait_for(recv.at[pl.ds(0, per - (n == 0))], a_recv.at[t, n])
        return p, recv[pl.ds(p * per, per)].reshape(per * 2 * CH, width)

    def in_lanes(part, pieces):
        rows = part.shape[0] // pieces
        return jnp.concatenate([part[i * rows : (i + 1) * rows] for i in range(pieces)], axis=1)

    def arrive(n):
        p, part = taken(0, recv0_s, n)
        here = pl.ds(pl.multiple_of(p * span, span), span)
        four = 4 * 2 * CH
        rows = four // ROWS
        o, i = iota((four, four), 0), iota((four, four), 1)
        order = (o % rows) // ROWS * CH + o // rows * ROWS + o % ROWS
        part = mm(one_hot(order == i), in_lanes(part, per // 4))
        total = None
        for r in range(ROWS):
            row = jnp.concatenate(
                [
                    part[r * rows : (r + 1) * rows, k * width : (k + 1) * width]
                    for k in range(per // 4)
                ],
                axis=0,
            )
            raw1_s[own + r, here, :] = row.astype(BF16)
            normed = ln(row, eg_ref[...])
            x_s[own + r, here, :] = normed
            term = nt(head_rows(eb_ref, r), normed)
            total = term if total is None else total + term
        piece = raw1_s.at[pl.ds(own, ROWS), here, :]
        remote(piece, piece, t_send.at[1], t_recv.at[2], partner).start()
        order = given(p * span + iota((count, span), 1))
        order = one_hot(iota((count, span), 0) == order)
        mask = mm(jnp.broadcast_to(mask_ref[...].astype(F32).astype(BF16), (CH, count)), order)
        bias1_s[x, yi, z, :, here] = (total * LOG2E + (mask - 1.0) * far_mask).astype(BF16)

    def drain(t, raw, bias, stage):
        wait_for(raw.at[pl.ds(own, ROWS)], t_send.at[t])
        wait_for(bias.at[0, 0, pl.ds(0, near - 1)], z_send.at[t])
        wait_for(part_of(bias, 0, 0), z_send.at[t])
        wait_for(bias.at[pl.ds(0, 3)], x_send.at[t])
        wait_for(stage.at[pl.ds(0, members - 1)], a_send.at[t])

    for r in range(ROWS):
        raw0_s[own + r] = pair_ref[r]
    v_s[:, :, width:] = jnp.ones((TEAM, count, width), BF16)
    total = None
    for r in range(ROWS):
        normed = ln(pair_ref[r].astype(F32), sg_ref[...])
        x_s[own + r] = normed
        term = nt(head_rows(sb_ref, r), normed)
        total = term if total is None else total + term
    mask = mask_ref[...].astype(F32)
    bias0_s[x, yi, z] = (total * LOG2E + (mask - 1.0) * far_mask).astype(BF16)
    pl.semaphore_wait(barrier, members)
    gather_plane(0, bias0_s)
    for i in range(2):
        rows = raw0_s.at[pl.ds(own + 2 * i, 2)]
        remote(rows, rows, t_send.at[0], t_recv.at[i], partner).start()

    update(0, sg_ref, sp_ref, so_ref, raw0_s, bias0_s, stage0_s, recv0_s, lambda: arrive(0))
    arrive(1)
    arrive(2)
    arrive(3)
    gather_plane(1, bias1_s)
    update(1, eg_ref, ep_ref, eo_ref, raw1_s, bias1_s, stage1_s, recv1_s, lambda: None)
    line = nz * 2 * CH
    rows = line // ROWS
    o, i = iota((line, line), 0), iota((line, line), 1)
    order = (o % rows) // ROWS
    order = ((order % nz) * 2 + order // nz) * CH + o // rows * ROWS + o % ROWS
    order = one_hot(order == i)
    for n in range(nx):
        p, part = taken(1, recv1_s, n)
        part = mm(order, in_lanes(part, nyi)).astype(BF16)
        for k in range(nyi):
            here = pl.ds(pl.multiple_of(p * span + k * group, group), group)
            for r in range(ROWS):
                out_ref[r, here, :] = part[
                    r * rows : (r + 1) * rows, k * width : (k + 1) * width
                ]
    drain(0, raw0_s, bias0_s, stage0_s)
    drain(1, raw1_s, bias1_s, stage1_s)


def solution(mesh):
    n = mesh.shape["row"]
    dims = (4, 4, n // 16)

    def body(pair, token_mask, sg, sp, sb, so, eg, ep, eb, eo):
        rows, count, width = pair.shape
        nx, ny, nz = dims
        near, members = ny // 2 * (nz // 2), n // 2
        quer, span = near * ROWS, 2 * near * TEAM
        tall = quer * HEADS
        vmem = pl.BlockSpec(memory_space=pltpu.VMEM)
        dma = pltpu.SemaphoreType.DMA
        return pl.pallas_call(
            functools.partial(kernel, dims),
            out_shape=jax.ShapeDtypeStruct(pair.shape, BF16),
            in_specs=[vmem] * 10,
            out_specs=vmem,
            scratch_shapes=[
                pltpu.VMEM((TEAM, count, width), BF16),
                pltpu.VMEM((TEAM, count, width), BF16),
                pltpu.VMEM((TEAM, count, width), BF16),
                pltpu.VMEM((TEAM, count, 2 * width), BF16),
                pltpu.VMEM((TEAM, nx, 2, tall, count), F32),
                pltpu.VMEM((TEAM, nx, 2 * quer, width), F32),
                pltpu.VMEM((TEAM, nx, 2 * quer, width), F32),
                pltpu.VMEM((ROWS, tall, count), BF16),
                pltpu.VMEM((ROWS, tall, width), F32),
                pltpu.VMEM((ROWS, tall, width), F32),
                pltpu.VMEM((quer * ROWS, width), F32),
                pltpu.VMEM((nx, ny // 2, nz, CH, count), BF16),
                pltpu.VMEM((nx, ny // 2, nz, CH, count), BF16),
                pltpu.VMEM((members, 2, CH, width), BF16),
                pltpu.VMEM((members, 2, CH, width), BF16),
                pltpu.VMEM((members, 2, CH, width), BF16),
                pltpu.VMEM((members, 2, CH, width), BF16),
                pltpu.VMEM((2 * quer, span), BF16),
                pltpu.VMEM((tall, quer), BF16),
                pltpu.VMEM((width, 2 * width), BF16),
                pltpu.VMEM((width, 2 * width), BF16),
                dma((2,)), dma((3,)), dma((2,)), dma((2, 2)),
                dma((2,)), dma((2, 8)), dma((2,)), dma((2, 4)),
            ],
            compiler_params=pltpu.CompilerParams(
                collective_id=0, has_side_effects=True, vmem_limit_bytes=60 * 1024 * 1024
            ),
        )(
            pair, token_mask.reshape(1, count), sg.reshape(1, width), sp, sb.T, so,
            eg.reshape(1, width), ep, eb.T, eo,
        )

    return jax.shard_map(
        body,
        mesh=mesh,
        in_specs=(P(("rep", "row"), None, None), P("rep"), P(), P(), P(), P(), P(), P(), P(), P()),
        out_specs=P(("rep", "row"), None, None),
        check_vma=False,
    )
```

time: 93.3 us -> 96.3 us (1.032)
  Pallas kernels: 91.3 us -> 94.2 us
    pallas_call x1, Pallas kernels: 91.3 us -> 94.2 us  [body(): pl.pallas_call(functools.partial(kernel, dims), out_shape=jax.ShapeDtypeS...]
where the time goes in v4:
time: 96.3 us; the launch traced here: 96.1 us
  Pallas kernels  94.2 us (98%)
  local copies, waits for them, and re-layouts  1.87 us (2%)
    pallas_call x1, Pallas kernels, body(): pl.pallas_call(functools.partial(kernel, dims), out_shape=jax.ShapeDtypeS...  94.2 us

profile of v4, /device:TPU:56, one launch (start us, length us, event | category | flops | bytes accessed | tf_op | source)
XLA Modules:
  0.0 96.1 jit_solution(16972994612929208564)
XLA Ops:
  0.0 94.2 %shard_map.100 = bf16[4,512,128]{2,1,0:T(8,128)(2,1)} custom-call(bf16[4,512,128]{2,1,0:T(8,128)(2,1)} %pair_ref.1, s32[1,512]{1,0:T(1,128)} %bitcast.5, f32[1,128]{1,0:T(1,128)} %bitcast.8, bf16[128,512]{1,0:T(8,128)(2,1)} %sp_ref.1, bf16[4,128]{1,0:T(4,128)(2,1)} %bitcast.6, bf16[128,128]{1,0:T(8,128)(2,1)} %so_ref.1, f32[1,128]{1,0:T(1,128)} %bitcast.9, ...), custom_call_target="tpu_custom_call" | custom-call | tf_op jit(solution)/shard_map/pallas_call | solution.py:388
  94.2 1.9 %copy.12 = bf16[4,512,128]{2,1,0:T(8,128)(2,1)} copy(bf16[4,512,128]{2,1,0:T(8,128)(2,1)} %shard_map.100) | data formatting | bytes 1048576

commit v5 on v4

--- a/solution.py
+++ b/solution.py
@@ -45,7 +45,7 @@
     pair_ref, mask_ref, sg_ref, sp_ref, sb_ref, so_ref, eg_ref, ep_ref, eb_ref, eo_ref,
     out_ref,
     raw0_s, raw1_s, x_s, v_s, score_s, gate_s, res_s, e_s, top_s, low_s, turn_s,
-    bias0_s, bias1_s, stage0_s, stage1_s, recv0_s, recv1_s, pick_s, spread_s, wkv_s, wqg_s,
+    bias0_s, bias1_s, stage0_s, stage1_s, recv0_s, recv1_s, pick_s, spread_s, wkv_s, wqg_s, q_s,
     t_send, t_recv, z_send, z_recv, x_send, x_recv, a_send, a_recv,
 ):
     nx, ny, nz = dims
@@ -61,7 +61,7 @@
     width = x_s.shape[2]
     count = x_s.shape[1]
     size = width // HEADS
-    quer = near * ROWS
+    quer = per * ROWS
     tall = quer * HEADS
     span = per * TEAM
     group = nz * TEAM
@@ -150,10 +150,9 @@
         wait_for(quarter(bias, far, 0, late), x_recv.at[t, 4 + late])
         wait_for(quarter(bias, far, 1, late), x_recv.at[t, 6 + late])
 
-    def update(t, g_ref, p_ref, o_ref, raw, bias, stage, recv, on_last):
-        row, col = iota((2 * quer, span), 0), iota((2 * quer, span), 1)
-        share = row // ROWS
-        token = place(0, share // near, share % near) * TEAM + ROWS * cls + row % ROWS
+    def update(t, g_ref, p_ref, o_ref, raw, bias, stage, recv):
+        row, col = iota((quer, span), 0), iota((quer, span), 1)
+        token = row // ROWS * TEAM + ROWS * cls + row % ROWS
         pick_s[...] = one_hot((given(token) if t == 0 else token) == col)
         wkv_s[...] = p_ref[:, width : 3 * width]
         wqg_s[:, :width] = p_ref[:, :width]
@@ -177,16 +176,14 @@
                 qg = mm(normed, wqg_s[...])
                 gate = jax.nn.sigmoid(qg[:, width:].astype(BF16).astype(F32))
                 q = (qg[:, :width] * (LOG2E / math.sqrt(size))).astype(BF16)
+                q = mm(spread_s[...], jnp.concatenate([q[:quer], q[quer:]], axis=1))
                 for n, k in enumerate(pair):
                     res_s[k, p] = both[:, (2 + n) * width : (3 + n) * width]
-                    gate_s[k, p] = gate[2 * n * quer : 2 * (n + 1) * quer]
-                for half in range(2):
-                    lo = half * quer
-                    two = [q[lo + 2 * n * quer : lo + (2 * n + 1) * quer] for n in range(2)]
-                    wide = mm(spread_s[...], jnp.concatenate(two, axis=1))
-                    for n, k in enumerate(pair):
-                        one = (wide[:, n * width : (n + 1) * width] * head).astype(BF16)
-                        score_s[k, p, half] = nt(one, keys[n])
+                    gate_s[k, p] = gate[n * quer : (n + 1) * quer]
+                    one = q[:, n * width : (n + 1) * width] * head
+                    q_s[n, p * tall : (p + 1) * tall, :] = one.astype(BF16)
+            for n, k in enumerate(pair):
+                score_s[k] = nt(q_s[n], keys[n]).reshape(nx, tall, count)
 
         def finish(i):
             for k in (i, i + 1):
@@ -197,53 +194,56 @@
         project(own + 2)
         wait_for(bias.at[0, 0, pl.ds(0, near - 1)], z_recv.at[t, 0])
         to_neighbours(t, bias, 0)
-        if t == 0:
-            wait_for(raw.at[pl.ds(other, 2)], t_recv.at[0])
-        else:
+        if t == 1:
             wait_for(raw.at[pl.ds(other, ROWS)], t_recv.at[2])
-        finish(other)
+            finish(other)
         wait_for(part_of(bias, 0, 0), z_recv.at[t, 1])
         to_neighbours(t, bias, 1)
+        if t == 1:
+            finish(other + 2)
 
         def unit(n, c):
-            @pl.when(n == 2)
-            def _():
-                relay(t, bias, 0)
-
-            @pl.when(n == 4)
-            def _():
-                if t == 0:
+            if t == 0:
+                rel = jnp.where(n < 6, n % 3, 3)
+                kind = jnp.where(n < 6, n // 3, n % 2)
+
+                @pl.when(n == 1)
+                def _():
+                    wait_for(raw.at[pl.ds(other, 2)], t_recv.at[0])
+                    finish(other)
+                    relay(t, bias, 0)
+                    relay(t, bias, 1)
+
+                @pl.when(n == 3)
+                def _():
                     wait_for(raw.at[pl.ds(other + 2, 2)], t_recv.at[1])
-                finish(other + 2)
-                relay(t, bias, 1)
-
-            @pl.when(n == 8)
+                    finish(other + 2)
+
+            else:
+                rel, kind = n // 2, n % 2
+
+                @pl.when(n == 2)
+                def _():
+                    relay(t, bias, 0)
+                    relay(t, bias, 1)
+
+            @pl.when(n == 6)
             def _():
                 from_far(t, bias, 0)
-
-            @pl.when(n == 14)
-            def _():
-                on_last()
                 from_far(t, bias, 1)
 
-            q = (n - 8) // 2
-            rel = jnp.where(n >= 8, jnp.where((q == 0) | (q == 3), 3, q), jnp.maximum(n % 4 - 1, 0))
-            late = jnp.where(n >= 8, (q > 0).astype(jnp.int32), (n % 4 == 1).astype(jnp.int32))
-            kind = jnp.where(n >= 8, n % 2, n // 4)
             p = lax.rem(x + (rel ^ (rel >> 1)), nx)
-            half = (hz + late) % 2
             side = (cls + kind) % 2
             base = ROWS * side
             for r in range(ROWS):
-                for k in range(near):
+                for k in range(per):
                     part = slice(k * CH, (k + 1) * CH)
-                    add = bias[p, k // nzh, half * nzh + k % nzh].astype(F32)
-                    s = score_s[base + r, p, half, part, :] + add
+                    add = bias[p, k // nz, k % nz].astype(F32)
+                    s = score_s[base + r, p, part, :] + add
                     e_s[r, part, :] = jnp.exp2(s - jnp.max(s, axis=-1, keepdims=True)).astype(BF16)
                 out = mm(e_s[r], v_s[base + r])
                 top_s[r] = out[:, :width]
                 low_s[r] = out[:, width:]
-            here = pl.ds(pl.multiple_of(half * quer, quer), quer)
             hid = []
             for r in range(ROWS):
                 top = top_s[r, pl.ds(0, quer, stride=HEADS), :]
@@ -252,39 +252,37 @@
                     rows = pl.ds(h, quer, stride=HEADS)
                     top = jnp.where(lane_head == h, top_s[r, rows, :], top)
                     low = jnp.where(lane_head == h, low_s[r, rows, :], low)
-                hid.append((gate_s[base + r, p, here, :] * (top / low)).astype(BF16))
+                hid.append((gate_s[base + r, p] * (top / low)).astype(BF16))
             u = mm(jnp.concatenate(hid, axis=0), o_ref[...])
             if t == 1:
                 u = u.astype(BF16).astype(F32)
             for r in range(ROWS):
                 turn_s[pl.ds(r, quer, stride=ROWS), :] = (
-                    res_s[base + r, p, here, :] + u[r * quer : (r + 1) * quer]
+                    res_s[base + r, p] + u[r * quer : (r + 1) * quer]
                 )
-            turned = turn_s[...].astype(BF16).reshape(near, CH, width)
-            for i in range(nyi):
-                stage[pl.ds(place(p, half, i * nzh), nzh), side] = turned[i * nzh : (i + 1) * nzh]
-
-            def send(k, c):
-                m = place(p, half, lax.rem(local + k, near))
-
-                @pl.when(m != mine)
-                def _():
-                    remote(
-                        stage.at[m, side], recv.at[mine, side], a_send.at[t], a_recv.at[t, rel],
-                        member(m),
-                    ).start()
-
-                return c
-
-            lax.fori_loop(0, near, send, 0)
-
-            @pl.when((n == 0) | (n == 4))
+            stage[pl.ds(p * per, per), side] = turn_s[...].astype(BF16).reshape(per, CH, width)
+
+            def send(k):
+                m = p * per + lax.rem(mine + k, per)
+                remote(
+                    stage.at[m, side], recv.at[mine, side], a_send.at[t], a_recv.at[t, rel],
+                    member(m),
+                ).start()
+
+            for k in range(1, per):
+                send(k)
+
+            @pl.when(rel == 0)
             def _():
                 recv[mine, side] = stage[mine, side]
 
+            @pl.when(rel > 0)
+            def _():
+                send(0)
+
             return c
 
-        lax.fori_loop(0, 16, unit, 0)
+        lax.fori_loop(0, 8, unit, 0)
 
     def taken(t, recv, n):
         p = (x, down, up, far)[n]
@@ -348,12 +346,13 @@
         rows = raw0_s.at[pl.ds(own + 2 * i, 2)]
         remote(rows, rows, t_send.at[0], t_recv.at[i], partner).start()
 
-    update(0, sg_ref, sp_ref, so_ref, raw0_s, bias0_s, stage0_s, recv0_s, lambda: arrive(0))
+    update(0, sg_ref, sp_ref, so_ref, raw0_s, bias0_s, stage0_s, recv0_s)
+    arrive(0)
     arrive(1)
     arrive(2)
     arrive(3)
     gather_plane(1, bias1_s)
-    update(1, eg_ref, ep_ref, eo_ref, raw1_s, bias1_s, stage1_s, recv1_s, lambda: None)
+    update(1, eg_ref, ep_ref, eo_ref, raw1_s, bias1_s, stage1_s, recv1_s)
     line = nz * 2 * CH
     rows = line // ROWS
     o, i = iota((line, line), 0), iota((line, line), 1)
@@ -381,7 +380,8 @@
         rows, count, width = pair.shape
         nx, ny, nz = dims
         near, members = ny // 2 * (nz // 2), n // 2
-        quer, span = near * ROWS, 2 * near * TEAM
+        per = 2 * near
+        quer, span = per * ROWS, per * TEAM
         tall = quer * HEADS
         vmem = pl.BlockSpec(memory_space=pltpu.VMEM)
         dma = pltpu.SemaphoreType.DMA
@@ -395,9 +395,9 @@
                 pltpu.VMEM((TEAM, count, width), BF16),
                 pltpu.VMEM((TEAM, count, width), BF16),
                 pltpu.VMEM((TEAM, count, 2 * width), BF16),
-                pltpu.VMEM((TEAM, nx, 2, tall, count), F32),
-                pltpu.VMEM((TEAM, nx, 2 * quer, width), F32),
-                pltpu.VMEM((TEAM, nx, 2 * quer, width), F32),
+                pltpu.VMEM((TEAM, nx, tall, count), F32),
+                pltpu.VMEM((TEAM, nx, quer, width), F32),
+                pltpu.VMEM((TEAM, nx, quer, width), F32),
                 pltpu.VMEM((ROWS, tall, count), BF16),
                 pltpu.VMEM((ROWS, tall, width), F32),
                 pltpu.VMEM((ROWS, tall, width), F32),
@@ -408,10 +408,11 @@
                 pltpu.VMEM((members, 2, CH, width), BF16),
                 pltpu.VMEM((members, 2, CH, width), BF16),
                 pltpu.VMEM((members, 2, CH, width), BF16),
-                pltpu.VMEM((2 * quer, span), BF16),
+                pltpu.VMEM((quer, span), BF16),
                 pltpu.VMEM((tall, quer), BF16),
                 pltpu.VMEM((width, 2 * width), BF16),
                 pltpu.VMEM((width, 2 * width), BF16),
+                pltpu.VMEM((2, nx * tall, width), BF16),
                 dma((2,)), dma((3,)), dma((2,)), dma((2, 2)),
                 dma((2,)), dma((2, 8)), dma((2,)), dma((2, 4)),
             ],

time: 96.3 us -> 82.1 us (0.85); the launches traced: 96.1 us -> 80.8 us
  Pallas kernels: 94.2 us -> 78.9 us
    pallas_call x1, Pallas kernels: 94.2 us -> 78.9 us  [body(): pl.pallas_call(functools.partial(kernel, dims), out_shape=jax.ShapeDtypeS...]
where the time goes in v5:
time: 82.1 us; the launch traced here: 80.8 us
  Pallas kernels  78.9 us (96%)
  local copies, waits for them, and re-layouts  1.87 us (2%)
    pallas_call x1, Pallas kernels, body(): pl.pallas_call(functools.partial(kernel, dims), out_shape=jax.ShapeDtypeS...  78.9 us
    unnamed x1, local copies, waits for them, and re-layouts  1.87 us

profile of v5, /device:TPU:56, one launch (start us, length us, event | category | flops | bytes accessed | tf_op | source)
XLA Modules:
  0.0 80.8 jit_solution(16646062022109251609)
XLA Ops:
  0.0 78.9 %shard_map.100 = bf16[4,512,128]{2,1,0:T(8,128)(2,1)} custom-call(bf16[4,512,128]{2,1,0:T(8,128)(2,1)} %pair_ref.1, s32[1,512]{1,0:T(1,128)} %bitcast.5, f32[1,128]{1,0:T(1,128)} %bitcast.8, bf16[128,512]{1,0:T(8,128)(2,1)} %sp_ref.1, bf16[4,128]{1,0:T(4,128)(2,1)} %bitcast.6, bf16[128,128]{1,0:T(8,128)(2,1)} %so_ref.1, f32[1,128]{1,0:T(1,128)} %bitcast.9, ...), custom_call_target="tpu_custom_call" | custom-call | tf_op jit(solution)/shard_map/pallas_call | solution.py:388
  78.9 1.9 %copy.12 = bf16[4,512,128]{2,1,0:T(8,128)(2,1)} copy(bf16[4,512,128]{2,1,0:T(8,128)(2,1)} %shard_map.100) | data formatting | bytes 1048576

commit v6 on v5

--- a/solution.py
+++ b/solution.py
@@ -45,7 +45,7 @@
     pair_ref, mask_ref, sg_ref, sp_ref, sb_ref, so_ref, eg_ref, ep_ref, eb_ref, eo_ref,
     out_ref,
     raw0_s, raw1_s, x_s, v_s, score_s, gate_s, res_s, e_s, top_s, low_s, turn_s,
-    bias0_s, bias1_s, stage0_s, stage1_s, recv0_s, recv1_s, pick_s, spread_s, wkv_s, wqg_s, q_s,
+    bias0_s, bias1_s, stage0_s, stage1_s, recv0_s, recv1_s, pick_s, spread_s, wkv_s, wqg_s, q_s, mask_s,
     t_send, t_recv, z_send, z_recv, x_send, x_recv, a_send, a_recv,
 ):
     nx, ny, nz = dims
@@ -99,7 +99,6 @@
         rest = token % group
         return token - rest + (rest // ROWS) % 2 * (nz * ROWS) + rest // TEAM * ROWS + rest % ROWS
 
-    spread_s[...] = one_hot(iota((tall, quer), 0) // HEADS == iota((tall, quer), 1))
     lane_head = iota((quer, width), 1) // size
     head = (iota((tall, width), 0) % HEADS == iota((tall, width), 1) // size).astype(F32)
     far_mask = 1e9 * LOG2E
@@ -150,7 +149,7 @@
         wait_for(quarter(bias, far, 0, late), x_recv.at[t, 4 + late])
         wait_for(quarter(bias, far, 1, late), x_recv.at[t, 6 + late])
 
-    def update(t, g_ref, p_ref, o_ref, raw, bias, stage, recv):
+    def constants(t, p_ref):
         row, col = iota((quer, span), 0), iota((quer, span), 1)
         token = row // ROWS * TEAM + ROWS * cls + row % ROWS
         pick_s[...] = one_hot((given(token) if t == 0 else token) == col)
@@ -158,6 +157,7 @@
         wqg_s[:, :width] = p_ref[:, :width]
         wqg_s[:, width:] = p_ref[:, 3 * width :]
 
+    def update(t, g_ref, o_ref, raw, bias, stage, recv):
         def project(i):
             pair = (i, i + 1)
             kv = [mm(x_s[k], wkv_s[...]) for k in pair]
@@ -317,10 +317,7 @@
             total = term if total is None else total + term
         piece = raw1_s.at[pl.ds(own, ROWS), here, :]
         remote(piece, piece, t_send.at[1], t_recv.at[2], partner).start()
-        order = given(p * span + iota((count, span), 1))
-        order = one_hot(iota((count, span), 0) == order)
-        mask = mm(jnp.broadcast_to(mask_ref[...].astype(F32).astype(BF16), (CH, count)), order)
-        bias1_s[x, yi, z, :, here] = (total * LOG2E + (mask - 1.0) * far_mask).astype(BF16)
+        bias1_s[x, yi, z, :, here] = (total * LOG2E + mask_s[:, here]).astype(BF16)
 
     def drain(t, raw, bias, stage):
         wait_for(raw.at[pl.ds(own, ROWS)], t_send.at[t])
@@ -329,9 +326,6 @@
         wait_for(bias.at[pl.ds(0, 3)], x_send.at[t])
         wait_for(stage.at[pl.ds(0, members - 1)], a_send.at[t])
 
-    for r in range(ROWS):
-        raw0_s[own + r] = pair_ref[r]
-    v_s[:, :, width:] = jnp.ones((TEAM, count, width), BF16)
     total = None
     for r in range(ROWS):
         normed = ln(pair_ref[r].astype(F32), sg_ref[...])
@@ -343,16 +337,25 @@
     pl.semaphore_wait(barrier, members)
     gather_plane(0, bias0_s)
     for i in range(2):
-        rows = raw0_s.at[pl.ds(own + 2 * i, 2)]
-        remote(rows, rows, t_send.at[0], t_recv.at[i], partner).start()
-
-    update(0, sg_ref, sp_ref, so_ref, raw0_s, bias0_s, stage0_s, recv0_s)
-    arrive(0)
-    arrive(1)
-    arrive(2)
-    arrive(3)
+        remote(
+            pair_ref.at[pl.ds(2 * i, 2)], raw0_s.at[pl.ds(own + 2 * i, 2)],
+            t_send.at[0], t_recv.at[i], partner,
+        ).start()
+    for r in range(ROWS):
+        raw0_s[own + r] = pair_ref[r]
+    v_s[:, :, width:] = jnp.ones((TEAM, count, width), BF16)
+    spread_s[...] = one_hot(iota((tall, quer), 0) // HEADS == iota((tall, quer), 1))
+    constants(0, sp_ref)
+
+    update(0, sg_ref, so_ref, raw0_s, bias0_s, stage0_s, recv0_s)
+    constants(1, ep_ref)
+    order = one_hot(iota((count, count), 0) == given(iota((count, count), 1)))
+    mask = mm(jnp.broadcast_to(mask_ref[...].astype(F32).astype(BF16), (CH, count)), order)
+    mask_s[...] = (mask - 1.0) * far_mask
+    for n in range(nx):
+        arrive(n)
     gather_plane(1, bias1_s)
-    update(1, eg_ref, ep_ref, eo_ref, raw1_s, bias1_s, stage1_s, recv1_s)
+    update(1, eg_ref, eo_ref, raw1_s, bias1_s, stage1_s, recv1_s)
     line = nz * 2 * CH
     rows = line // ROWS
     o, i = iota((line, line), 0), iota((line, line), 1)
@@ -361,7 +364,7 @@
     order = one_hot(order == i)
     for n in range(nx):
         p, part = taken(1, recv1_s, n)
-        part = mm(order, in_lanes(part, nyi)).astype(BF16)
+        part = mm(order, in_lanes(part, nyi))
         for k in range(nyi):
             here = pl.ds(pl.multiple_of(p * span + k * group, group), group)
             for r in range(ROWS):
@@ -387,7 +390,7 @@
         dma = pltpu.SemaphoreType.DMA
         return pl.pallas_call(
             functools.partial(kernel, dims),
-            out_shape=jax.ShapeDtypeStruct(pair.shape, BF16),
+            out_shape=jax.ShapeDtypeStruct(pair.shape, F32),
             in_specs=[vmem] * 10,
             out_specs=vmem,
             scratch_shapes=[
@@ -413,6 +416,7 @@
                 pltpu.VMEM((width, 2 * width), BF16),
                 pltpu.VMEM((width, 2 * width), BF16),
                 pltpu.VMEM((2, nx * tall, width), BF16),
+                pltpu.VMEM((CH, count), F32),
                 dma((2,)), dma((3,)), dma((2,)), dma((2, 2)),
                 dma((2,)), dma((2, 8)), dma((2,)), dma((2, 4)),
             ],
@@ -422,7 +426,7 @@
         )(
             pair, token_mask.reshape(1, count), sg.reshape(1, width), sp, sb.T, so,
             eg.reshape(1, width), ep, eb.T, eo,
-        )
+        ).astype(BF16)
 
     return jax.shard_map(
         body,

time: 82.1 us -> 82.7 us (level)
  other arithmetic: 0 us -> 2.09 us
  local copies, waits for them, and re-layouts: 1.87 us -> 0 us
    convert_element_type x0 -> x1, other arithmetic: none -> 2.09 us  [body(): return pl.pallas_call(functools.partial(kernel, dims), out_shape=jax.Shap...]
    unnamed x1 -> x0, local copies, waits for them, and re-layouts: 1.87 us -> none
where the time goes in v6:
time: 82.7 us; the launch traced here: 81.3 us
  Pallas kernels  79.2 us (96%)
  other arithmetic  2.09 us (3%)
    pallas_call x1, Pallas kernels, body(): pl.pallas_call(functools.partial(kernel, dims), out_shape=jax.ShapeDtypeS...  79.2 us
    convert_element_type x1, other arithmetic, body(): return pl.pallas_call(functools.partial(kernel, dims), out_shape=jax.Shap...  2.09 us

profile of v6, /device:TPU:56, one launch (start us, length us, event | category | flops | bytes accessed | tf_op | source)
XLA Modules:
  0.0 81.3 jit_solution(14788278546257390649)
XLA Ops:
  0.0 79.2 %shard_map.100 = f32[4,512,128]{2,1,0:T(8,128)} custom-call(bf16[4,512,128]{2,1,0:T(8,128)(2,1)} %pair_ref.1, s32[1,512]{1,0:T(1,128)} %bitcast.5, f32[1,128]{1,0:T(1,128)} %bitcast.8, bf16[128,512]{1,0:T(8,128)(2,1)} %sp_ref.1, bf16[4,128]{1,0:T(4,128)(2,1)} %bitcast.6, bf16[128,128]{1,0:T(8,128)(2,1)} %so_ref.1, f32[1,128]{1,0:T(1,128)} %bitcast.9, ...), custom_call_target="tpu_custom_call" | custom-call | tf_op jit(solution)/shard_map/pallas_call | solution.py:391
  79.2 2.1 %convert_element_type.3 = bf16[4,512,128]{2,1,0:T(8,128)(2,1)} convert(f32[4,512,128]{2,1,0:T(8,128)} %shard_map.100) | non-fusion elementwise | flops 262144 | bytes 1572864 | tf_op jit(solution)/shard_map/convert_element_type | solution.py:429

commit v7 on v6

--- a/solution.py
+++ b/solution.py
@@ -42,8 +42,9 @@
 
 def kernel(
     dims,
-    pair_ref, mask_ref, sg_ref, sp_ref, sb_ref, so_ref, eg_ref, ep_ref, eb_ref, eo_ref,
+    pair_in, mask_in, sg_in, sp_in, sb_in, so_in, eg_in, ep_in, eb_in, eo_in,
     out_ref,
+    mask_ref, sg_ref, sp_ref, sb_ref, so_ref, eg_ref, ep_ref, eb_ref, eo_ref, load_sem,
     raw0_s, raw1_s, x_s, v_s, score_s, gate_s, res_s, e_s, top_s, low_s, turn_s,
     bias0_s, bias1_s, stage0_s, stage1_s, recv0_s, recv1_s, pick_s, spread_s, wkv_s, wqg_s, q_s, mask_s,
     t_send, t_recv, z_send, z_recv, x_send, x_recv, a_send, a_recv,
@@ -66,6 +67,18 @@
     span = per * TEAM
     group = nz * TEAM
 
+    own = ROWS * cls
+    other = ROWS - own
+    own_rows = raw0_s.at[pl.ds(own, ROWS)]
+    loads = (
+        (pair_in, own_rows), (sg_in, sg_ref), (sb_in, sb_ref), (mask_in, mask_ref),
+        (sp_in, sp_ref), (so_in, so_ref), (eg_in, eg_ref), (ep_in, ep_ref), (eb_in, eb_ref),
+        (eo_in, eo_ref),
+    )
+    loads = [pltpu.make_async_copy(a, b, load_sem.at[i]) for i, (a, b) in enumerate(loads)]
+    for load in loads:
+        load.start()
+
     barrier = pltpu.get_barrier_semaphore()
 
     def greet_one(peer):
@@ -103,8 +116,6 @@
     head = (iota((tall, width), 0) % HEADS == iota((tall, width), 1) // size).astype(F32)
     far_mask = 1e9 * LOG2E
 
-    own = ROWS * cls
-    other = ROWS - own
     up, down, far = lax.rem(x + 1, nx), lax.rem(x + nx - 1, nx), lax.rem(x + 2, nx)
     to_up = member(mine + (up - x) * per)
     to_down = member(mine + (down - x) * per)
@@ -326,9 +337,11 @@
         wait_for(bias.at[pl.ds(0, 3)], x_send.at[t])
         wait_for(stage.at[pl.ds(0, members - 1)], a_send.at[t])
 
+    for load in loads[:4]:
+        load.wait()
     total = None
     for r in range(ROWS):
-        normed = ln(pair_ref[r].astype(F32), sg_ref[...])
+        normed = ln(raw0_s[own + r].astype(F32), sg_ref[...])
         x_s[own + r] = normed
         term = nt(head_rows(sb_ref, r), normed)
         total = term if total is None else total + term
@@ -337,12 +350,10 @@
     pl.semaphore_wait(barrier, members)
     gather_plane(0, bias0_s)
     for i in range(2):
-        remote(
-            pair_ref.at[pl.ds(2 * i, 2)], raw0_s.at[pl.ds(own + 2 * i, 2)],
-            t_send.at[0], t_recv.at[i], partner,
-        ).start()
-    for r in range(ROWS):
-        raw0_s[own + r] = pair_ref[r]
+        rows = raw0_s.at[pl.ds(own + 2 * i, 2)]
+        remote(rows, rows, t_send.at[0], t_recv.at[i], partner).start()
+    for load in loads[4:]:
+        load.wait()
     v_s[:, :, width:] = jnp.ones((TEAM, count, width), BF16)
     spread_s[...] = one_hot(iota((tall, quer), 0) // HEADS == iota((tall, quer), 1))
     constants(0, sp_ref)
@@ -364,7 +375,7 @@
     order = one_hot(order == i)
     for n in range(nx):
         p, part = taken(1, recv1_s, n)
-        part = mm(order, in_lanes(part, nyi))
+        part = mm(order, in_lanes(part, nyi)).astype(BF16)
         for k in range(nyi):
             here = pl.ds(pl.multiple_of(p * span + k * group, group), group)
             for r in range(ROWS):
@@ -390,10 +401,22 @@
         dma = pltpu.SemaphoreType.DMA
         return pl.pallas_call(
             functools.partial(kernel, dims),
-            out_shape=jax.ShapeDtypeStruct(pair.shape, F32),
-            in_specs=[vmem] * 10,
+            out_shape=jax.ShapeDtypeStruct(pair.shape, BF16),
+            in_specs=[pl.BlockSpec(memory_space=pl.ANY)] * 10,
             out_specs=vmem,
             scratch_shapes=[
+                pltpu.VMEM((1, count), jnp.int32),
+                *[
+                    shape
+                    for _ in range(2)
+                    for shape in (
+                        pltpu.VMEM((1, width), F32),
+                        pltpu.VMEM((width, 4 * width), BF16),
+                        pltpu.VMEM((HEADS, width), BF16),
+                        pltpu.VMEM((width, width), BF16),
+                    )
+                ],
+                dma((10,)),
                 pltpu.VMEM((TEAM, count, width), BF16),
                 pltpu.VMEM((TEAM, count, width), BF16),
                 pltpu.VMEM((TEAM, count, width), BF16),
@@ -426,7 +449,7 @@
         )(
             pair, token_mask.reshape(1, count), sg.reshape(1, width), sp, sb.T, so,
             eg.reshape(1, width), ep, eb.T, eo,
-        ).astype(BF16)
+        )
 
     return jax.shard_map(
         body,

time: 82.7 us -> 81.2 us (0.982); the launches traced: 81.3 us -> 80.7 us
  other arithmetic: 2.09 us -> 0 us
  local copies, waits for them, and re-layouts: 0 us -> 1.87 us
    convert_element_type x1 -> x0, other arithmetic: 2.09 us -> none  [body(): return pl.pallas_call(functools.partial(kernel, dims), out_shape=jax.Shap...]
    unnamed x0 -> x1, local copies, waits for them, and re-layouts: none -> 1.87 us
where the time goes in v7:
time: 81.2 us; the launch traced here: 80.7 us
  Pallas kernels  78.8 us (97%)
  local copies, waits for them, and re-layouts  1.87 us (2%)
    pallas_call x1, Pallas kernels, body(): pl.pallas_call(functools.partial(kernel, dims), out_shape=jax.ShapeDtypeS...  78.8 us
    unnamed x1, local copies, waits for them, and re-layouts  1.87 us

profile of v7, /device:TPU:56, one launch (start us, length us, event | category | flops | bytes accessed | tf_op | source)
XLA Modules:
  0.0 80.7 jit_solution(12394017873543401896)
XLA Ops:
  0.0 78.8 %shard_map.100 = bf16[4,512,128]{2,1,0:T(8,128)(2,1)} custom-call(bf16[4,512,128]{2,1,0:T(8,128)(2,1)} %pair_in.1, s32[1,512]{1,0:T(1,128)} %bitcast.5, f32[1,128]{1,0:T(1,128)} %bitcast.8, bf16[128,512]{1,0:T(8,128)(2,1)} %sp_in.1, bf16[4,128]{1,0:T(4,128)(2,1)} %bitcast.6, bf16[128,128]{1,0:T(8,128)(2,1)} %so_in.1, f32[1,128]{1,0:T(1,128)} %bitcast.9, ...), custom_call_target="tpu_custom_call" | custom-call | tf_op jit(solution)/shard_map/pallas_call | solution.py:402
  78.8 1.9 %copy.12 = bf16[4,512,128]{2,1,0:T(8,128)(2,1)} copy(bf16[4,512,128]{2,1,0:T(8,128)(2,1)} %shard_map.100) | data formatting | bytes 1048576

commit v8 on v7

--- a/solution.py
+++ b/solution.py
@@ -46,7 +46,7 @@
     out_ref,
     mask_ref, sg_ref, sp_ref, sb_ref, so_ref, eg_ref, ep_ref, eb_ref, eo_ref, load_sem,
     raw0_s, raw1_s, x_s, v_s, score_s, gate_s, res_s, e_s, top_s, low_s, turn_s,
-    bias0_s, bias1_s, stage0_s, stage1_s, recv0_s, recv1_s, pick_s, spread_s, wkv_s, wqg_s, q_s, mask_s,
+    bias0_s, bias1_s, stage0_s, stage1_s, recv0_s, recv1_s, pick_s, spread_s, wkv_s, wqg_s, q_s, mask_s, total_s,
     t_send, t_recv, z_send, z_recv, x_send, x_recv, a_send, a_recv,
 ):
     nx, ny, nz = dims
@@ -109,8 +109,10 @@
         pltpu.make_async_copy(view, view, sem).wait()
 
     def given(token):
-        rest = token % group
-        return token - rest + (rest // ROWS) % 2 * (nz * ROWS) + rest // TEAM * ROWS + rest % ROWS
+        rest = token % span
+        share = rest % quer // ROWS
+        line = share // nz * group + share % nz * ROWS + rest % ROWS
+        return token - rest + line + rest // quer * (nz * ROWS)
 
     lane_head = iota((quer, width), 1) // size
     head = (iota((tall, width), 0) % HEADS == iota((tall, width), 1) // size).astype(F32)
@@ -162,7 +164,7 @@
 
     def constants(t, p_ref):
         row, col = iota((quer, span), 0), iota((quer, span), 1)
-        token = row // ROWS * TEAM + ROWS * cls + row % ROWS
+        token = cls * quer + row
         pick_s[...] = one_hot((given(token) if t == 0 else token) == col)
         wkv_s[...] = p_ref[:, width : 3 * width]
         wqg_s[:, :width] = p_ref[:, :width]
@@ -240,6 +242,9 @@
 
             @pl.when(n == 6)
             def _():
+                if t == 0:
+                    for k in range(3):
+                        arrive(k, 0)
                 from_far(t, bias, 0)
                 from_far(t, bias, 1)
 
@@ -276,7 +281,7 @@
             def send(k):
                 m = p * per + lax.rem(mine + k, per)
                 remote(
-                    stage.at[m, side], recv.at[mine, side], a_send.at[t], a_recv.at[t, rel],
+                    stage.at[m, side], recv.at[mine, side], a_send.at[t], a_recv.at[t, 2 * rel + kind],
                     member(m),
                 ).start()
 
@@ -295,39 +300,45 @@
 
         lax.fori_loop(0, 8, unit, 0)
 
-    def taken(t, recv, n):
-        p = (x, down, up, far)[n]
-        wait_for(recv.at[pl.ds(0, per - (n == 0))], a_recv.at[t, n])
-        return p, recv[pl.ds(p * per, per)].reshape(per * 2 * CH, width)
-
-    def in_lanes(part, pieces):
-        rows = part.shape[0] // pieces
-        return jnp.concatenate([part[i * rows : (i + 1) * rows] for i in range(pieces)], axis=1)
-
-    def arrive(n):
-        p, part = taken(0, recv0_s, n)
-        here = pl.ds(pl.multiple_of(p * span, span), span)
-        four = 4 * 2 * CH
-        rows = four // ROWS
-        o, i = iota((four, four), 0), iota((four, four), 1)
-        order = (o % rows) // ROWS * CH + o // rows * ROWS + o % ROWS
-        part = mm(one_hot(order == i), in_lanes(part, per // 4))
+    def taken(t, recv, n, kind):
+        p, side = (x, down, up, far)[n], (cls + kind) % 2
+        wait_for(recv.at[pl.ds(0, per - (n == 0)), 0], a_recv.at[t, 2 * n + kind])
+        part = recv[pl.ds(p * per, per), side].reshape(per * CH, width)
+        line = nz * CH
+        part = [part[i * line : (i + 1) * line] for i in range(nyi)]
+        o, i = iota((line, line), 0), iota((line, line), 1)
+        rows = nz * ROWS
+        order = one_hot(o % rows // ROWS * CH + o // rows * ROWS + o % ROWS == i)
+        return p, side, mm(order, jnp.concatenate(part, axis=1))
+
+    def arrive(n, kind):
+        p, side, part = taken(0, recv0_s, n, kind)
+        here = pl.ds(pl.multiple_of(p * span + side * quer, quer), quer)
+        rows = nz * ROWS
         total = None
         for r in range(ROWS):
+            row = part[r * rows : (r + 1) * rows]
             row = jnp.concatenate(
-                [
-                    part[r * rows : (r + 1) * rows, k * width : (k + 1) * width]
-                    for k in range(per // 4)
-                ],
-                axis=0,
+                [row[:, k * width : (k + 1) * width] for k in range(nyi)], axis=0
             )
             raw1_s[own + r, here, :] = row.astype(BF16)
             normed = ln(row, eg_ref[...])
             x_s[own + r, here, :] = normed
             term = nt(head_rows(eb_ref, r), normed)
             total = term if total is None else total + term
+        total_s[n, kind] = total
         piece = raw1_s.at[pl.ds(own, ROWS), here, :]
         remote(piece, piece, t_send.at[1], t_recv.at[2], partner).start()
+
+    def share_of_plane(n):
+        p = (x, down, up, far)[n]
+        here = pl.ds(pl.multiple_of(p * span, span), span)
+        first, second = total_s[n, 0], total_s[n, 1]
+        total = jnp.where(
+            cls == 0,
+            jnp.concatenate([first, second], axis=1),
+            jnp.concatenate([second, first], axis=1),
+        )
         bias1_s[x, yi, z, :, here] = (total * LOG2E + mask_s[:, here]).astype(BF16)
 
     def drain(t, raw, bias, stage):
@@ -364,24 +375,23 @@
     mask = mm(jnp.broadcast_to(mask_ref[...].astype(F32).astype(BF16), (CH, count)), order)
     mask_s[...] = (mask - 1.0) * far_mask
     for n in range(nx):
-        arrive(n)
+        if n == 3:
+            arrive(n, 0)
+        arrive(n, 1)
+        share_of_plane(n)
     gather_plane(1, bias1_s)
     update(1, eg_ref, eo_ref, raw1_s, bias1_s, stage1_s, recv1_s)
-    line = nz * 2 * CH
-    rows = line // ROWS
-    o, i = iota((line, line), 0), iota((line, line), 1)
-    order = (o % rows) // ROWS
-    order = ((order % nz) * 2 + order // nz) * CH + o // rows * ROWS + o % ROWS
-    order = one_hot(order == i)
     for n in range(nx):
-        p, part = taken(1, recv1_s, n)
-        part = mm(order, in_lanes(part, nyi)).astype(BF16)
-        for k in range(nyi):
-            here = pl.ds(pl.multiple_of(p * span + k * group, group), group)
-            for r in range(ROWS):
-                out_ref[r, here, :] = part[
-                    r * rows : (r + 1) * rows, k * width : (k + 1) * width
-                ]
+        for kind in range(2):
+            p, side, part = taken(1, recv1_s, n, kind)
+            part = part.astype(BF16)
+            rows = nz * ROWS
+            for k in range(nyi):
+                here = pl.ds(pl.multiple_of(p * span + k * group + side * rows, rows), rows)
+                for r in range(ROWS):
+                    out_ref[r, here, :] = part[
+                        r * rows : (r + 1) * rows, k * width : (k + 1) * width
+                    ]
     drain(0, raw0_s, bias0_s, stage0_s)
     drain(1, raw1_s, bias1_s, stage1_s)
 
@@ -440,8 +450,9 @@
                 pltpu.VMEM((width, 2 * width), BF16),
                 pltpu.VMEM((2, nx * tall, width), BF16),
                 pltpu.VMEM((CH, count), F32),
+                pltpu.VMEM((nx, 2, CH, quer), F32),
                 dma((2,)), dma((3,)), dma((2,)), dma((2, 2)),
-                dma((2,)), dma((2, 8)), dma((2,)), dma((2, 4)),
+                dma((2,)), dma((2, 8)), dma((2,)), dma((2, 8)),
             ],
             compiler_params=pltpu.CompilerParams(
                 collective_id=0, has_side_effects=True, vmem_limit_bytes=60 * 1024 * 1024

time: 81.2 us -> 80.8 us (level)
  no operation moved by 1% of the time
where the time goes in v8:
time: 80.8 us; the launch traced here: 80.2 us
  Pallas kernels  78.3 us (97%)
  local copies, waits for them, and re-layouts  1.87 us (2%)
    pallas_call x1, Pallas kernels, body(): pl.pallas_call(functools.partial(kernel, dims), out_shape=jax.ShapeDtypeS...  78.3 us
    unnamed x1, local copies, waits for them, and re-layouts  1.87 us

profile of v8, /device:TPU:56, one launch (start us, length us, event | category | flops | bytes accessed | tf_op | source)
XLA Modules:
  0.0 80.2 jit_solution(7463575703453071701)
XLA Ops:
  0.0 78.3 %shard_map.100 = bf16[4,512,128]{2,1,0:T(8,128)(2,1)} custom-call(bf16[4,512,128]{2,1,0:T(8,128)(2,1)} %pair_in.1, s32[1,512]{1,0:T(1,128)} %bitcast.5, f32[1,128]{1,0:T(1,128)} %bitcast.8, bf16[128,512]{1,0:T(8,128)(2,1)} %sp_in.1, bf16[4,128]{1,0:T(4,128)(2,1)} %bitcast.6, bf16[128,128]{1,0:T(8,128)(2,1)} %so_in.1, f32[1,128]{1,0:T(1,128)} %bitcast.9, ...), custom_call_target="tpu_custom_call" | custom-call | tf_op jit(solution)/shard_map/pallas_call | solution.py:412
  78.3 1.9 %copy.12 = bf16[4,512,128]{2,1,0:T(8,128)(2,1)} copy(bf16[4,512,128]{2,1,0:T(8,128)(2,1)} %shard_map.100) | data formatting | bytes 1048576

commit v9 on v8

--- a/solution.py
+++ b/solution.py
@@ -93,11 +93,13 @@
     partner = me + nz * (1 - 2 * cls)
     greet_one(partner)
 
-    def greet(s, c):
-        greet_one(member(lax.rem(mine + s, members)))
-        return c
-
-    lax.fori_loop(1, members, greet, 0)
+    along_z = [lax.rem(z + k, nz) for k in range(nz)]
+    for i in range(nx):
+        for j in range(nyi):
+            line = (lax.rem(x + i, nx) * ny + 2 * lax.rem(yi + j, nyi) + cls) * nz
+            for k in range(nz):
+                if i + j + k > 0:
+                    greet_one(line + along_z[k])
 
     def remote(src, dst, send, recv, peer):
         return pltpu.make_async_remote_copy(
@@ -137,13 +139,10 @@
     def gather_plane(t, bias):
         for late in range(2):
 
-            def go(s, c):
+            for s in range(1 - late, near):
                 peer = member(place(x, (hz + late) % 2, lax.rem(local + s, near)))
                 share = bias.at[x, yi, z]
                 remote(share, share, z_send.at[t], z_recv.at[t, late], peer).start()
-                return c
-
-            lax.fori_loop(1 - late, near, go, 0)
 
     def to_neighbours(t, bias, late):
         part = part_of(bias, x, late)

time: 80.8 us -> 80.6 us (level)
  no operation moved by 1% of the time
where the time goes in v9:
time: 80.6 us; the launch traced here: 79.8 us
  Pallas kernels  78 us (97%)
  local copies, waits for them, and re-layouts  1.87 us (2%)
    pallas_call x1, Pallas kernels, body(): pl.pallas_call(functools.partial(kernel, dims), out_shape=jax.ShapeDtypeS...  78 us
    unnamed x1, local copies, waits for them, and re-layouts  1.87 us

profile of v9, /device:TPU:56, one launch (start us, length us, event | category | flops | bytes accessed | tf_op | source)
XLA Modules:
  0.0 79.8 jit_solution(779143080315140340)
XLA Ops:
  0.0 78.0 %shard_map.100 = bf16[4,512,128]{2,1,0:T(8,128)(2,1)} custom-call(bf16[4,512,128]{2,1,0:T(8,128)(2,1)} %pair_in.1, s32[1,512]{1,0:T(1,128)} %bitcast.5, f32[1,128]{1,0:T(1,128)} %bitcast.8, bf16[128,512]{1,0:T(8,128)(2,1)} %sp_in.1, bf16[4,128]{1,0:T(4,128)(2,1)} %bitcast.6, bf16[128,128]{1,0:T(8,128)(2,1)} %so_in.1, f32[1,128]{1,0:T(1,128)} %bitcast.9, ...), custom_call_target="tpu_custom_call" | custom-call | tf_op jit(solution)/shard_map/pallas_call | solution.py:411
  78.0 1.9 %copy.12 = bf16[4,512,128]{2,1,0:T(8,128)(2,1)} copy(bf16[4,512,128]{2,1,0:T(8,128)(2,1)} %shard_map.100) | data formatting | bytes 1048576
